TPU v7x, 32 devices: a whole 2x2x4 slice. The times are simulated.
32 devices in a mesh: ga: 2 (over x), gy: 8 (over z, y), gx: 2 (over core).
Axes of the slice: x: 2, y: 2, z: 4, core: 2. Of those that a mesh axis runs over, the one named last changes fastest.
Arguments:
- inputs: bfloat16 [2, 32, 8192], P(None, 'ga'), parts along dimension 1, may hold values from -6 to 6
- norm_gain: bfloat16 [8192], replicated, may hold values from 0.099609375 to 1.8984375
- w_query: bfloat16 [8192, 8192], P('gx', 'gy'), may hold values from -0.0625 to 0.0625
- w_key: bfloat16 [8192, 1024], P('gx', 'gy'), may hold values from -0.0625 to 0.0625
- w_value: bfloat16 [8192, 1024], P('gx', 'gy'), may hold values from -0.0625 to 0.0625
- output_weight: bfloat16 [8192, 8192], P('gx', 'gy'), may hold values from -1.5 to 1.5
- cache_keys: bfloat16 [32, 4096, 1024], P('ga', 'gy', 'gx'), parts along dimension 0, may hold values from -810 to 810
- cache_values: bfloat16 [32, 4096, 1024], P('ga', 'gy', 'gx'), parts along dimension 0, may hold values from -6 to 6
- lengths: int32 [32], P('ga'), parts along dimension 0, may hold values from 1024 to 4096, as said below
Outputs:
- mixed: bfloat16 [2, 32, 8192], P(None, 'ga', ('gy', 'gx')), parts along dimension 1
- fresh_kv: bfloat16 [2, 32, 2, 1024], P(None, 'ga', None, 'gx'), parts along dimension 1
There are 2 independent parts, one for each index of `ga`. A program takes and returns all parts, laid end to end along the dimension named above; an argument that names none is the same for every part. Nothing has to cross between parts.
Inputs may be any that keep to these rules, and one draw needn't show every extreme that they name: Row b's cache holds valid entries at positions below lengths[b]; some row of every group fills all 4096 positions.
All inputs are finite; a program needn't handle non-finite values.
Results may differ from a plain program's by a relative error of at most 0.012.
The roundings to bfloat16 on the way count: a program that leaves them out, or rounds other values in their place, can miss the bound.
Values may be sent and summed in bfloat16 or wider, within the bound.
A program may use at most 128 MiB of HBM per device.

v0:
```python
import math

import jax
import jax.numpy as jnp
from jax import lax
from jax.sharding import PartitionSpec as P

HQ = 64
KV = 8
HD = 128


THETA = 500000.0
EPS = 1e-05


def rotate(values, positions):
    half_width = values.shape[-1] // 2
    frequency = jnp.exp(
        jnp.arange(half_width, dtype=jnp.float32) * (-2.0 * math.log(THETA) / values.shape[-1])
    )
    angles = positions[..., None, None] * frequency
    cos_part = jnp.cos(angles)
    sine_part = jnp.sin(angles)
    first_half = values[..., :half_width]
    second_half = values[..., half_width:]
    return jnp.concatenate(
        [
            first_half * cos_part - second_half * sine_part,
            second_half * cos_part + first_half * sine_part,
        ],
        axis=-1,
    )


def on_device(
    inputs, norm_gain, w_query, w_key, w_value, output_weight, cache_keys, cache_values, lengths
):
    n_gx = lax.axis_size("gx")
    gx_pos = lax.axis_index("gx")
    gy_pos = lax.axis_index("gy")
    steps_total = inputs.shape[0]
    batch_rows = inputs.shape[1]
    input_half_width = w_query.shape[0]
    cache_span = cache_keys.shape[1]
    kv_local = cache_keys.shape[2]
    heads_kv = kv_local // HD
    group_size = HQ // KV
    heads_here = heads_kv * group_size
    q_width = heads_here * HD
    output_columns = output_weight.shape[1]
    own_cols = output_columns // n_gx
    score_scale = HD ** (-0.5)
    states = inputs.astype(jnp.float32)
    normalized_input = (
        states
        * lax.rsqrt(jnp.mean(states * states, axis=-1, keepdims=True) + EPS)
        * norm_gain.astype(jnp.float32)
    ).astype(jnp.bfloat16)
    normed_local = lax.dynamic_slice_in_dim(
        normalized_input, gx_pos * input_half_width, input_half_width, 2
    )
    residual_cols = lax.dynamic_slice_in_dim(
        states, gy_pos * output_columns + gx_pos * own_cols, own_cols, 2
    )
    offsets = gy_pos * cache_span + jnp.arange(cache_span, dtype=jnp.int32)
    valid_mask = offsets[None, :] < lengths[:, None]
    keys_here = cache_keys.reshape(batch_rows, cache_span, heads_kv, HD)
    values_here = cache_values.reshape(batch_rows, cache_span, heads_kv, HD)
    prior_keys = jnp.zeros((0, batch_rows, kv_local), jnp.bfloat16)
    prior_values = jnp.zeros((0, batch_rows, kv_local), jnp.bfloat16)
    mixed_list = []
    fresh_list = []
    for step_index in range(steps_total):
        block = normed_local[step_index : step_index + 1]
        q_part = jnp.einsum("cbd,de->cbe", block, w_query, preferred_element_type=jnp.float32)
        k_part = jnp.einsum("cbd,de->cbe", block, w_key, preferred_element_type=jnp.float32)
        v_part = jnp.einsum("cbd,de->cbe", block, w_value, preferred_element_type=jnp.float32)
        q_sum, k_sum, v_sum = lax.psum((q_part, k_part, v_part), "gx")
        positions = (
            lengths.astype(jnp.float32)[None, :]
            + (step_index + jnp.arange(1, dtype=jnp.float32))[:, None]
        )
        q_rot = (
            rotate(q_sum.reshape(1, batch_rows, -1, HD), positions)
            .astype(jnp.bfloat16)
            .reshape(1, batch_rows, -1)
        )
        query_all = lax.all_gather(q_rot, "gy", axis=2, tiled=True)
        keys_all = lax.all_gather(k_sum.astype(jnp.bfloat16), "gy", axis=2, tiled=True)
        values_all = lax.all_gather(v_sum.astype(jnp.bfloat16), "gy", axis=2, tiled=True)
        query_mine = lax.dynamic_slice_in_dim(query_all, gx_pos * q_width, q_width, 2)
        keys_raw = lax.dynamic_slice_in_dim(keys_all, gx_pos * kv_local, kv_local, 2)
        values_new = lax.dynamic_slice_in_dim(values_all, gx_pos * kv_local, kv_local, 2)
        keys_new = (
            rotate(keys_raw.astype(jnp.float32).reshape(1, batch_rows, heads_kv, HD), positions)
            .astype(jnp.bfloat16)
            .reshape(1, batch_rows, kv_local)
        )
        fresh_block = jnp.stack([keys_new, values_new], axis=2)
        keys_seen = jnp.concatenate([prior_keys, keys_new], axis=0)
        values_seen = jnp.concatenate([prior_values, values_new], axis=0)
        visible_token_count = keys_seen.shape[0]
        queries = query_mine.reshape(1, batch_rows, heads_kv, group_size, HD)
        cache_score = (
            jnp.einsum("cbkgd,bpkd->cbkgp", queries, keys_here, preferred_element_type=jnp.float32)
            * score_scale
        )
        cache_score = jnp.where(valid_mask[None, :, None, None, :], cache_score, -jnp.inf)
        fresh_score = (
            jnp.einsum(
                "cbkgd,jbkd->cbkgj",
                queries,
                keys_seen.reshape(visible_token_count, batch_rows, heads_kv, HD),
                preferred_element_type=jnp.float32,
            )
            * score_scale
        )
        causal = (
            jnp.arange(visible_token_count, dtype=jnp.int32)[None, :]
            <= (step_index + jnp.arange(1, dtype=jnp.int32))[:, None]
        )
        fresh_score = jnp.where(causal[:, None, None, None, :], fresh_score, -jnp.inf)
        local_peak = jnp.maximum(jnp.max(cache_score, axis=-1), jnp.max(fresh_score, axis=-1))
        peak_score = lax.pmax(local_peak, "gy")
        cache_weight = jnp.exp(cache_score - peak_score[..., None])
        fresh_weight = jnp.exp(fresh_score - peak_score[..., None])
        cache_total = jnp.sum(cache_weight, axis=-1).reshape(1, batch_rows, heads_here)
        fresh_total = jnp.sum(fresh_weight, axis=-1).reshape(1, batch_rows, heads_here)
        cache_acc = jnp.einsum(
            "cbkgp,bpkd->cbkgd",
            cache_weight.astype(jnp.bfloat16),
            values_here,
            preferred_element_type=jnp.float32,
        )
        fresh_acc = jnp.einsum(
            "cbkgj,jbkd->cbkgd",
            fresh_weight.astype(jnp.bfloat16),
            values_seen.reshape(visible_token_count, batch_rows, heads_kv, HD),
            preferred_element_type=jnp.float32,
        )
        cache_acc = cache_acc.reshape(1, batch_rows, heads_here, HD)
        fresh_acc = fresh_acc.reshape(1, batch_rows, heads_here, HD)
        acc_sum, total_sum = lax.psum((cache_acc, cache_total), "gy")
        attention_result = ((acc_sum + fresh_acc) / (total_sum + fresh_total)[..., None]).astype(
            jnp.bfloat16
        )
        attention_result = attention_result.reshape(1, batch_rows, q_width)
        output_piece = jnp.einsum(
            "yjz,zo->yjo", attention_result, output_weight, preferred_element_type=jnp.float32
        )
        projected = lax.psum_scatter(output_piece, "gx", scatter_dimension=2, tiled=True)
        mixed_block = (residual_cols[step_index : step_index + 1] + projected).astype(jnp.bfloat16)
        mixed_block, fresh_block, prior_keys, prior_values = (
            mixed_block,
            fresh_block,
            keys_seen,
            values_seen,
        )
        mixed_list.append(mixed_block)
        fresh_list.append(fresh_block)
    mixed_all = jnp.concatenate(mixed_list, axis=0)
    fresh_all = jnp.concatenate(fresh_list, axis=0)
    return (mixed_all, fresh_all)


def solution(mesh):
    return jax.shard_map(
        on_device,
        mesh=mesh,
        in_specs=(
            P(None, "ga", None),
            P(),
            P("gx", "gy"),
            P("gx", "gy"),
            P("gx", "gy"),
            P("gx", "gy"),
            P("ga", "gy", "gx"),
            P("ga", "gy", "gx"),
            P("ga"),
        ),
        out_specs=(P(None, "ga", ("gy", "gx")), P(None, "ga", None, "gx")),
        check_vma=False,
    )
```

profile of v0, /device:TPU:0, one launch (start us, length us, event | category | flops | bytes accessed | tf_op | source)
XLA Modules:
  0.0 388.7 jit_solution(11195342151354800550)
XLA Ops:
  7.2 1.2 convert_element_type.125
  8.4 1.6 multiply_reduce_fusion
  10.0 0.7 dynamic-slice.1
  10.8 0.1 fusion.57
  10.9 4.7 %convolution_bitcast_fusion.4 = f32[2,8,8,128]{3,1,2,0:T(8,128)S(1)} fusion(bf16[4096,1024]{1,0:T(8,128)(2,1)} %param.11, bf16[2,16,4096]{2,1,0:T(8,128)(2,1)S(1)} %fusion.57), kind=kOutput, calls=%fused_computation.31 | convolution fusion | flops 134217728 | bytes 8585216 | tf_op jit(solution)/shard_map/cbd,de->cbe/dot_general | solution.py:76
  15.7 1.0 slice-done.1
  16.7 1.2 convolution_bitcast_fusion.2
  17.9 0.6 copy.77
  18.5 0.6 copy.80
  19.2 0.2 convolution_bitcast_fusion.5
  19.5 0.3 convolution_bitcast_fusion.7
  19.7 0.3 convolution_bitcast_fusion.6
  20.0 0.3 convolution_bitcast_fusion.8
  20.3 3.7 all-reduce.3
  24.0 27.5 %all_gather.23 = bf16[1,16,1024]{2,1,0:T(8,128)(2,1)S(1)} all-gather(bf16[1,16,128]{2,1,0:T(8,128)(2,1)S(1)} %get-tuple-element.17), channel_id=1, replica_groups=mesh['ga'=2,'gy'=8,'gx'=2] {'gy'}, dimensions={2}, use_global_device_ids=true | all-gather | bytes 36864 | tf_op jit(solution)/shard_map/all_gather | solution.py:91
  51.5 26.0 %all_gather.19 = bf16[1,16,1024]{2,1,0:T(8,128)(2,1)S(1)} all-gather(bf16[1,16,128]{2,1,0:T(8,128)(2,1)S(1)} %get-tuple-element.16), channel_id=1, replica_groups=mesh['ga'=2,'gy'=8,'gx'=2] {'gy'}, dimensions={2}, use_global_device_ids=true | all-gather | bytes 36864 | tf_op jit(solution)/shard_map/all_gather | solution.py:90
  77.5 26.0 %all_gather.22 = bf16[1,16,1024]{2,1,0:T(8,128)(2,1)S(1)} all-gather(bf16[1,16,128]{2,1,0:T(8,128)(2,1)S(1)} %get-tuple-element.15), channel_id=1, replica_groups=mesh['ga'=2,'gy'=8,'gx'=2] {'gy'}, dimensions={2}, use_global_device_ids=true | all-gather | bytes 36864 | tf_op jit(solution)/shard_map/all_gather | solution.py:90
  103.6 0.1 multiply_cosine_fusion.1
  103.7 0.2 multiply_subtract_fusion
  104.0 0.2 fusion.82
  104.2 26.0 %all_gather.20 = bf16[1,16,1024]{2,1,0:T(8,128)(2,1)S(1)} all-gather(bf16[1,16,128]{2,1,0:T(8,128)(2,1)S(1)} %get-tuple-element.14), channel_id=1, replica_groups=mesh['ga'=2,'gy'=8,'gx'=2] {'gy'}, dimensions={2}, use_global_device_ids=true | all-gather | bytes 36864 | tf_op jit(solution)/shard_map/all_gather | solution.py:91
  130.4 0.2 fusion.83
  130.6 1.0 subtract_convert_fusion.1
  131.7 30.7 %all_gather.18 = bf16[1,16,8192]{2,1,0:T(8,128)(2,1)S(1)} all-gather(bf16[1,16,1024]{2,1,0:T(8,128)(2,1)S(1)} %convert_element_type.129), channel_id=1, replica_groups=mesh['ga'=2,'gy'=8,'gx'=2] {'gy'}, dimensions={2}, use_global_device_ids=true | all-gather | bytes 294912 | tf_op jit(solution)/shard_map/all_gather | solution.py:89
  162.5 1.0 subtract_convert_fusion
  163.5 0.1 pad_maximum_fusion.1
  163.6 30.8 %all_gather.21 = bf16[1,16,8192]{2,1,0:T(8,128)(2,1)S(1)} all-gather(bf16[1,16,1024]{2,1,0:T(8,128)(2,1)S(1)} %convert_element_type.136), channel_id=1, replica_groups=mesh['ga'=2,'gy'=8,'gx'=2] {'gy'}, dimensions={2}, use_global_device_ids=true | all-gather | bytes 294912 | tf_op jit(solution)/shard_map/all_gather | solution.py:89
  194.5 0.2 fusion.77
  194.7 5.8 %fusion.86 = (f32[16,4,8]{2,1,0:T(4,128)S(1)}, f32[1,16,4,8,512]{4,3,2,1,0:T(8,128)S(1)}) fusion(bf16[16,4,8,128]{3,2,1,0:T(8,128)(2,1)S(1)} %bitcast.227, pred[16,512]{1,0:T(8,128)(4,1)S(1)} %broadcast_compare_fusion, bf16[16,512,512]{2,1,0:T(8,128)(2,1)} %param.15), kind=kOutput, calls=%fused_computation.122 | convolution fusion | flops 67894784 | bytes 9578496 | tf_op jit(solution)/shard_map/cbkgd,bpkd->cbkgp/dot_general | solution.py:106
  200.5 5.8 %fusion.84 = (f32[16,4,8]{2,1,0:T(4,128)S(1)}, f32[1,16,4,8,512]{4,3,2,1,0:T(8,128)S(1)}) fusion(bf16[16,4,8,128]{3,2,1,0:T(8,128)(2,1)S(1)} %bitcast.224, pred[16,512]{1,0:T(8,128)(4,1)S(1)} %broadcast_compare_fusion, bf16[16,512,512]{2,1,0:T(8,128)(2,1)} %param.15), kind=kOutput, calls=%fused_computation.120 | convolution fusion | flops 67894784 | bytes 9578496 | tf_op jit(solution)/shard_map/cbkgd,bpkd->cbkgp/dot_general | solution.py:106
  206.2 0.3 fusion.85
  206.5 33.6 %all-reduce.2 = (f32[16,4,8]{2,1,0:T(4,128)S(1)}, f32[16,4,8]{2,1,0:T(4,128)S(1)}) all-reduce(f32[16,4,8]{2,1,0:T(4,128)S(1)} %max.28, f32[16,4,8]{2,1,0:T(4,128)S(1)} %multiply_maximum_fusion), channel_id=1, replica_groups=mesh['ga'=2,'gy'=8,'gx'=2] {'gy'}, use_global_device_ids=true, to_apply=%region_14.15 | all-reduce | flops 1024 | bytes 8192 | tf_op jit(solution)/shard_map/pmax | solution.py:125
  240.1 0.4 fusion.48
  240.5 5.4 %fusion.36 = f32[1,16,32,128]{3,2,1,0:T(8,128)} fusion(f32[1,16,4,8,512]{4,3,2,1,0:T(8,128)S(1)} %get-tuple-element.47, f32[16,4,8]{2,1,0:T(4,128)S(1)} %get-tuple-element.13, bf16[16,512,512]{2,1,0:T(8,128)(2,1)} %param.16), kind=kOutput, calls=%fused_computation.20 | convolution fusion | flops 67633152 | bytes 9701376 | tf_op jit(solution)/shard_map/cbkgp,bpkd->cbkgd/dot_general | solution.py:130
  245.9 0.4 fusion.50
  246.2 5.3 %fusion.39 = f32[1,16,32,128]{3,2,1,0:T(8,128)} fusion(f32[1,16,4,8,512]{4,3,2,1,0:T(8,128)S(1)} %get-tuple-element.43, f32[16,4,8]{2,1,0:T(4,128)S(1)} %get-tuple-element.12, bf16[16,512,512]{2,1,0:T(8,128)(2,1)} %param.16), kind=kOutput, calls=%fused_computation.21 | convolution fusion | flops 67633152 | bytes 9701376 | tf_op jit(solution)/shard_map/cbkgp,bpkd->cbkgd/dot_general | solution.py:130
  251.6 0.1 fusion.66
  251.9 34.7 %all-reduce = (f32[1,16,32]{1,2,0:T(8,128)S(1)}, f32[1,16,32]{1,2,0:T(8,128)S(1)}) all-reduce(f32[1,16,32]{1,2,0:T(8,128)S(1)} %bitcast.238, f32[1,16,32]{1,2,0:T(8,128)S(1)} %bitcast.237), channel_id=1, replica_groups=mesh['ga'=2,'gy'=8,'gx'=2] {'gy'}, use_global_device_ids=true, to_apply=%region_18.19 | all-reduce | flops 1024 | bytes 8192 | tf_op jit(solution)/shard_map/psum | solution.py:144
  287.0 69.7 %all-reduce.8.cloned.1.call-done = (f32[1,16,32,128]{3,2,1,0:T(8,128)}, f32[1,16,32,128]{3,2,1,0:T(8,128)}) async-done(((f32[1,16,32,128]{3,2,1,0:T(8,128)}, f32[1,16,32,128]{3,2,1,0:T(8,128)}), (f32[1,16,32,128]{3,2,1,0:T(8,128)}, f32[1,16,32,128]{3,2,1,0:T(8,128)})) %all-reduce.8.cloned.1.call-update) | async-done | bytes 524304 | tf_op jit(solution)/shard_map/psum | solution.py:144
  356.7 1.2 fusion.44
  357.9 5.2 %convolution_bitcast_fusion.1 = f32[1,16,1024]{2,1,0:T(8,128)} fusion(bf16[4096,1024]{1,0:T(8,128)(2,1)} %param.14, bf16[2,8,32,128]{3,2,1,0:T(8,128)(2,1)S(1)} %bitcast.228), kind=kOutput, calls=%fused_computation.26 | convolution fusion | flops 134217728 | bytes 8585216 | tf_op jit(solution)/shard_map/yjz,zo->yjo/dot_general | solution.py:149
  363.3 0.2 fusion.61
  363.5 5.2 %convolution_bitcast_fusion.3 = f32[1,16,1024]{2,1,0:T(8,128)} fusion(bf16[4096,1024]{1,0:T(8,128)(2,1)} %param.14, bf16[2,8,32,128]{3,2,1,0:T(8,128)(2,1)S(1)} %bitcast.223), kind=kOutput, calls=%fused_computation.30 | convolution fusion | flops 134217728 | bytes 8585216 | tf_op jit(solution)/shard_map/yjz,zo->yjo/dot_general | solution.py:149
  368.8 0.7 copy.72
  369.5 0.5 reduce-scatter.5.cloned.1.call-done
  370.0 10.8 %reduce-scatter.3.cloned.1.call-done = f32[1,16,512]{2,1,0:T(8,128)} async-done(((f32[1,16,1024]{2,1,0:T(8,128)}), f32[1,16,512]{2,1,0:T(8,128)}) %reduce-scatter.3.cloned.1.call-update) | async-done | bytes 32784 | tf_op jit(solution)/shard_map/reduce_scatter | solution.py:152
  380.8 0.8 fusion.71
  381.6 0.6 pad_maximum_fusion.3
  (64 shorter events, 1.3 us)
Async XLA Ops:
  7.2 12.1 %copy-start = (bf16[4096,128]{1,0:T(8,128)(2,1)S(1)}, bf16[4096,128]{1,0:T(8,128)(2,1)}, u32[]{:S(2)}) copy-start(bf16[4096,128]{1,0:T(8,128)(2,1)} %param.13) | copy-start | bytes 3145732
  7.2 123.4 %all-reduce.10.cloned.1.call-start = ((), (), s32[]{:S(2)}) async-start(), calls=%async_computation.5 | async-start | bytes 262144 | tf_op jit(solution)/shard_map/psum | solution.py:79
  8.4 2.5 copy-start.2
  10.8 4.9 %slice-start = ((s8[8388608]{0:T(1024)(128)(4,1)}), s8[4194304]{0:T(1024)(128)(4,1)S(1)}, s32[]{:S(2)}) async-start(s8[8388608]{0:T(1024)(128)(4,1)} %bitcast.221), calls=%async_computation.6 | async-start | bytes 8388608
  10.9 5.8 %slice-start.1 = ((s8[8388608]{0:T(1024)(128)(4,1)}), s8[4194304]{0:T(1024)(128)(4,1)S(1)}, s32[]{:S(2)}) async-start(s8[8388608]{0:T(1024)(128)(4,1)} %bitcast.221), calls=%async_computation.7 | async-start | bytes 8388608
  16.7 3.1 copy-start.1
  16.7 3.6 copy-start.4
  19.2 337.5 %all-reduce.8.cloned.1.call-start = ((), (), s32[]{:S(2)}) async-start(), calls=%async_computation.4 | async-start | bytes 1048576 | tf_op jit(solution)/shard_map/psum | solution.py:144
  286.7 83.3 %reduce-scatter.5.cloned.1.call-start = ((), (), s32[]{:S(2)}) async-start(), calls=%async_computation.3 | async-start | bytes 98304 | tf_op jit(solution)/shard_map/reduce_scatter | solution.py:152
  357.9 5.3 %copy-start.3 = (f32[1,16,32,128]{3,2,1,0:T(8,128)S(1)}, f32[1,16,32,128]{3,2,1,0:T(8,128)}, u32[]{:S(2)}) copy-start(f32[1,16,32,128]{3,2,1,0:T(8,128)} %get-tuple-element.11) | copy-start | bytes 786436
  363.2 17.6 %reduce-scatter.3.cloned.1.call-start = ((), (), s32[]{:S(2)}) async-start(), calls=%async_computation.2 | async-start | bytes 98304 | tf_op jit(solution)/shard_map/reduce_scatter | solution.py:152
Sparse Core Ops, SparseCore 0:
  19.3 20.6 all-reduce.9
  286.8 69.8 all-reduce.7
  363.3 6.6 reduce-scatter.4
  372.1 8.5 reduce-scatter.2
where the time goes:
time: 389 us
  blocking collectives  239 us (61%)
  waiting for transfers between devices  81.1 us (21%)
  matrix products  41.3 us (11%)
  between operations  14.1 us (4%)
  other arithmetic  8.65 us (2%)
  local copies, waits for them, and re-layouts  4.43 us (1%)
    psum x1, waiting for transfers between devices, on_device(): acc_sum, total_sum = lax.psum((cache_acc, cache_total), 'gy')  69.7 us
    all_gather x2, blocking collectives, on_device(): query_all = lax.all_gather(q_rot, 'gy', axis=2, tiled=True)  61.6 us
    all_gather x2, blocking collectives, on_device(): lax.all_gather(v_sum.astype(jnp.bfloat16), 'gy', axis=2, tiled=True)  53.5 us
    all_gather x2, blocking collectives, on_device(): lax.all_gather(k_sum.astype(jnp.bfloat16), 'gy', axis=2, tiled=True)  52 us
    psum x1, blocking collectives, on_device(): acc_sum, total_sum = lax.psum((cache_acc, cache_total), 'gy')  34.7 us
    pmax x1, blocking collectives, on_device(): peak_score = lax.pmax(local_peak, 'gy')  33.6 us
    dot_general x2, matrix products, on_device(): jnp.einsum('cbkgd,bpkd->cbkgp', queries, keys_here, preferred_element_typ...  11.5 us
    reduce_scatter x2, waiting for transfers between devices, on_device(): lax.psum_scatter(output_piece, 'gx', scatter_dimension=2, tiled=True)  11.3 us
  transfers between devices with their start and end apart: 4, of which 3 were waited for; matrix products, arithmetic and copies ran while one was open for 2% of the time, Pallas kernels for 0%

commit v1 on v0

v1 whole, which is shorter than its diff:
```python
import math

import jax
import jax.numpy as jnp
from jax import lax
from jax.sharding import PartitionSpec as P

HQ = 64
KV = 8
HD = 128


THETA = 500000.0
EPS = 1e-05


def rotate(values, positions):
    half_width = values.shape[-1] // 2
    frequency = jnp.exp(
        jnp.arange(half_width, dtype=jnp.float32) * (-2.0 * math.log(THETA) / values.shape[-1])
    )
    angles = positions[..., None, None] * frequency
    cos_part = jnp.cos(angles)
    sine_part = jnp.sin(angles)
    first_half = values[..., :half_width]
    second_half = values[..., half_width:]
    return jnp.concatenate(
        [
            first_half * cos_part - second_half * sine_part,
            second_half * cos_part + first_half * sine_part,
        ],
        axis=-1,
    )


def on_device_plain(
    inputs, norm_gain, w_query, w_key, w_value, output_weight, cache_keys, cache_values, lengths
):
    n_gx = lax.axis_size("gx")
    gx_pos = lax.axis_index("gx")
    gy_pos = lax.axis_index("gy")
    steps_total = inputs.shape[0]
    batch_rows = inputs.shape[1]
    input_half_width = w_query.shape[0]
    cache_span = cache_keys.shape[1]
    kv_local = cache_keys.shape[2]
    heads_kv = kv_local // HD
    group_size = HQ // KV
    heads_here = heads_kv * group_size
    q_width = heads_here * HD
    output_columns = output_weight.shape[1]
    own_cols = output_columns // n_gx
    score_scale = HD ** (-0.5)
    states = inputs.astype(jnp.float32)
    normalized_input = (
        states
        * lax.rsqrt(jnp.mean(states * states, axis=-1, keepdims=True) + EPS)
        * norm_gain.astype(jnp.float32)
    ).astype(jnp.bfloat16)
    block = lax.dynamic_slice_in_dim(
        normalized_input, gx_pos * input_half_width, input_half_width, 2
    )
    residual_cols = lax.dynamic_slice_in_dim(
        states, gy_pos * output_columns + gx_pos * own_cols, own_cols, 2
    )
    offsets = gy_pos * cache_span + jnp.arange(cache_span, dtype=jnp.int32)
    valid_mask = offsets[None, :] < lengths[:, None]
    keys_here = cache_keys.reshape(batch_rows, cache_span, heads_kv, HD)
    values_here = cache_values.reshape(batch_rows, cache_span, heads_kv, HD)
    q_part = jnp.einsum("cbd,de->cbe", block, w_query, preferred_element_type=jnp.float32)
    k_part = jnp.einsum("cbd,de->cbe", block, w_key, preferred_element_type=jnp.float32)
    v_part = jnp.einsum("cbd,de->cbe", block, w_value, preferred_element_type=jnp.float32)
    q_sum, k_sum, v_sum = lax.psum((q_part, k_part, v_part), "gx")
    positions = (
        lengths.astype(jnp.float32)[None, :]
        + jnp.arange(steps_total, dtype=jnp.float32)[:, None]
    )
    gather = lambda a: lax.all_gather(a, "gy", axis=2, tiled=True)
    mine = lambda a, width: lax.dynamic_slice_in_dim(a, gx_pos * width, width, 2)
    q_all = gather(
        q_sum.astype(jnp.float32)
        if q_sum.shape[2] % HD
        else rotate(q_sum.reshape(steps_total, batch_rows, -1, HD), positions)
        .astype(jnp.bfloat16)
        .reshape(q_sum.shape)
    )
    queries = mine(q_all, q_width).reshape(steps_total, batch_rows, heads_kv, group_size, HD)
    if q_sum.shape[2] % HD:
        queries = rotate(
            queries.reshape(steps_total, batch_rows, -1, HD), positions
        ).astype(jnp.bfloat16).reshape(queries.shape)
    keys_raw = mine(gather(k_sum.astype(jnp.bfloat16)), kv_local)
    values_new = mine(gather(v_sum.astype(jnp.bfloat16)), kv_local)
    keys_new = (
        rotate(keys_raw.astype(jnp.float32).reshape(steps_total, batch_rows, heads_kv, HD), positions)
        .astype(jnp.bfloat16)
        .reshape(steps_total, batch_rows, kv_local)
    )
    fresh_all = jnp.stack([keys_new, values_new], axis=2)
    cache_score = (
        jnp.einsum("cbkgd,bpkd->bkcgp", queries, keys_here, preferred_element_type=jnp.float32)
        * score_scale
    )
    cache_score = jnp.where(valid_mask[:, None, None, None, :], cache_score, -jnp.inf)
    fresh_score = (
        jnp.einsum(
            "cbkgd,jbkd->bkcgj",
            queries,
            keys_new.reshape(steps_total, batch_rows, heads_kv, HD),
            preferred_element_type=jnp.float32,
        )
        * score_scale
    )
    order = jnp.arange(steps_total, dtype=jnp.int32)
    causal = order[None, :] <= order[:, None]
    fresh_score = jnp.where(causal[:, None, :], fresh_score, -jnp.inf)
    local_peak = jnp.maximum(jnp.max(cache_score, axis=-1), jnp.max(fresh_score, axis=-1))
    peak_score = lax.pmax(local_peak, "gy")
    cache_weight = jnp.exp(cache_score - peak_score[..., None])
    fresh_weight = jnp.exp(fresh_score - peak_score[..., None])
    cache_total = jnp.sum(cache_weight, axis=-1)
    fresh_total = jnp.sum(fresh_weight, axis=-1)
    cache_acc = jnp.einsum(
        "bkcgp,bpkd->bkcgd",
        cache_weight.astype(jnp.bfloat16),
        values_here,
        preferred_element_type=jnp.float32,
    )
    fresh_acc = jnp.einsum(
        "bkcgj,jbkd->bkcgd",
        fresh_weight.astype(jnp.bfloat16),
        values_new.reshape(steps_total, batch_rows, heads_kv, HD),
        preferred_element_type=jnp.float32,
    )
    acc_sum, total_sum = lax.psum((cache_acc, cache_total), "gy")
    attention_result = ((acc_sum + fresh_acc) / (total_sum + fresh_total)[..., None]).astype(
        jnp.bfloat16
    )
    attention_result = jnp.transpose(attention_result, (2, 0, 1, 3, 4)).reshape(
        steps_total, batch_rows, q_width
    )
    output_piece = jnp.einsum(
        "yjz,zo->yjo", attention_result, output_weight, preferred_element_type=jnp.float32
    )
    projected = lax.psum_scatter(output_piece, "gx", scatter_dimension=2, tiled=True)
    mixed_all = (residual_cols + projected).astype(jnp.bfloat16)
    return (mixed_all, fresh_all)


def solution(mesh):
    return jax.shard_map(
        on_device_plain,
        mesh=mesh,
        in_specs=(
            P(None, "ga", None),
            P(),
            P("gx", "gy"),
            P("gx", "gy"),
            P("gx", "gy"),
            P("gx", "gy"),
            P("ga", "gy", "gx"),
            P("ga", "gy", "gx"),
            P("ga"),
        ),
        out_specs=(P(None, "ga", ("gy", "gx")), P(None, "ga", None, "gx")),
        check_vma=False,
    )
```

time: 389 us -> 273 us (0.70)
  blocking collectives: 239 us -> 158 us
  waiting for transfers between devices: 81.1 us -> 40.8 us
  local copies, waits for them, and re-layouts: 4.43 us -> 26.9 us
  matrix products: 41.3 us -> 25.4 us
    all_gather x6 -> x3, blocking collectives: 167 us -> 84.9 us  [on_device_plain(): gather = lambda a: lax.all_gather(a, 'gy', axis=2, tiled=True)]
    psum x2, waiting for transfers between devices: 69.7 us -> 34.6 us  [the longest x1 34.6 us: on_device_plain(): acc_sum, total_sum = lax.psum((cache_acc, cache_total), 'gy')]
    reshape x3 -> x5, local copies, waits for them, and re-layouts: 0.05 us -> 25.2 us  [the longest x1 12.5 us: on_device_plain(): values_here = cache_values.reshape(batch_rows, cache_span, heads_kv, HD)]
    dot_general x15 -> x8, matrix products: 41.3 us -> 25.4 us  [the longest x1 5.78 us: on_device_plain(): jnp.einsum('cbkgd,bpkd->bkcgp', queries, keys_here, preferred_element_typ...]
    reduce_scatter x2 -> x1, waiting for transfers between devices: 11.3 us -> 6.18 us  [on_device_plain(): lax.psum_scatter(output_piece, 'gx', scatter_dimension=2, tiled=True)]
  transfers between devices with their start and end apart: 4 -> 3, of which waited for: 3 -> 2; matrix products, arithmetic and copies ran while one was open for 2% -> 10% of each run, Pallas kernels for 0% -> 0%
where the time goes in v1:
time: 273 us; the launch traced here: 272 us
  blocking collectives  158 us (58%)
  waiting for transfers between devices  40.8 us (15%)
  local copies, waits for them, and re-layouts  26.9 us (10%)
  matrix products  25.4 us (9%)
  between operations  14.1 us (5%)
  other arithmetic  6.87 us (3%)
    all_gather x3, blocking collectives, on_device_plain(): gather = lambda a: lax.all_gather(a, 'gy', axis=2, tiled=True)  84.9 us
    psum x1, waiting for transfers between devices, on_device_plain(): acc_sum, total_sum = lax.psum((cache_acc, cache_total), 'gy')  34.6 us
    psum x1, blocking collectives, on_device_plain(): acc_sum, total_sum = lax.psum((cache_acc, cache_total), 'gy')  34.5 us
    pmax x1, blocking collectives, on_device_plain(): peak_score = lax.pmax(local_peak, 'gy')  34.5 us
    reshape x1, local copies, waits for them, and re-layouts, on_device_plain(): values_here = cache_values.reshape(batch_rows, cache_span, heads_kv, HD)  12.5 us
    reshape x1, local copies, waits for them, and re-layouts, on_device_plain(): keys_here = cache_keys.reshape(batch_rows, cache_span, heads_kv, HD)  12.5 us
    reduce_scatter x1, waiting for transfers between devices, on_device_plain(): lax.psum_scatter(output_piece, 'gx', scatter_dimension=2, tiled=True)  6.18 us
    dot_general x1, matrix products, on_device_plain(): jnp.einsum('cbkgd,bpkd->bkcgp', queries, keys_here, preferred_element_typ...  5.78 us
  transfers between devices with their start and end apart: 3, of which 2 were waited for; matrix products, arithmetic and copies ran while one was open for 10% of the time, Pallas kernels for 0%

profile of v1, /device:TPU:0, one launch (start us, length us, event | category | flops | bytes accessed | tf_op | source)
XLA Modules:
  0.0 271.8 jit_solution(2879689406997758738)
XLA Ops:
  7.2 0.0 copy-start
  7.2 0.0 copy-start.3
  7.2 0.0 all-reduce.4.cloned.1.call-start
  7.2 1.3 multiply_reduce_fusion
  8.5 1.1 convert_element_type.49
  9.7 0.0 copy-done.3
  9.7 0.1 fusion.25
  9.9 0.0 copy-start.4
  9.9 0.0 copy-start.2
  9.9 5.1 %fusion.6 = f32[2,16,1024]{2,1,0:T(8,128)S(1)} fusion(bf16[2,16,4096]{2,1,0:T(8,128)(2,1)S(1)} %fusion.25, bf16[4096,1024]{1,0:T(8,128)(2,1)} %param.11), kind=kOutput, calls=%fused_computation.6 | convolution fusion | flops 268435456 | bytes 8781824 | tf_op jit(solution)/shard_map/cbd,de->cbe/dot_general | solution.py:70
  15.0 0.7 copy.53
  15.7 0.0 all-reduce.4.cloned.1.call-update
  15.7 0.0 all-reduce.6.cloned.1.call-start
  15.8 0.0 copy-done.4
  15.9 0.1 broadcast_compare_fusion
  15.9 0.1 multiply_cosine_fusion
  16.1 0.3 fusion.18
  16.4 0.0 copy-done.2
  16.4 0.3 fusion.16
  16.7 3.7 %all-reduce = (bf16[2,16,128]{2,1,0:T(8,128)(2,1)S(1)}, bf16[2,16,128]{2,1,0:T(8,128)(2,1)S(1)}) all-reduce(f32[2,16,128]{2,1,0:T(8,128)S(1)} %fusion.18, f32[2,16,128]{2,1,0:T(8,128)S(1)} %fusion.16), channel_id=1, replica_groups=mesh['ga'=2,'gy'=8,'gx'=2] {'gx'}, use_global_device_ids=true, to_apply=%region_3.0 | all-reduce | flops 8192 | bytes 49152 | tf_op jit(solution)/shard_map/psum | solution.py:73
  20.4 27.5 %all_gather.10 = bf16[2,16,1024]{2,1,0:T(8,128)(2,1)S(1)} all-gather(bf16[2,16,128]{2,1,0:T(8,128)(2,1)S(1)} %get-tuple-element.6), channel_id=1, replica_groups=mesh['ga'=2,'gy'=8,'gx'=2] {'gy'}, dimensions={2}, use_global_device_ids=true | all-gather | bytes 73728 | tf_op jit(solution)/shard_map/all_gather | solution.py:78
  47.9 26.0 %all_gather.11 = bf16[2,16,1024]{2,1,0:T(8,128)(2,1)S(1)} all-gather(bf16[2,16,128]{2,1,0:T(8,128)(2,1)S(1)} %get-tuple-element.7), channel_id=1, replica_groups=mesh['ga'=2,'gy'=8,'gx'=2] {'gy'}, dimensions={2}, use_global_device_ids=true | all-gather | bytes 73728 | tf_op jit(solution)/shard_map/all_gather | solution.py:78
  74.0 0.1 fusion.36
  74.1 0.1 multiply_subtract_fusion
  74.2 12.5 %reshape.115 = bf16[16,512,4,128]{3,2,1,0:T(4,128)(2,1)} reshape(bf16[16,512,512]{2,1,0:T(8,128)(2,1)} %param.15) | data formatting | bytes 16777216 | tf_op jit(solution)/shard_map/reshape | solution.py:68
  86.7 12.5 %reshape.118 = bf16[16,512,4,128]{3,2,1,0:T(4,128)(2,1)} reshape(bf16[16,512,512]{2,1,0:T(8,128)(2,1)} %param.16) | data formatting | bytes 16777216 | tf_op jit(solution)/shard_map/reshape | solution.py:69
  99.3 0.1 maximum_convert_fusion
  99.4 0.0 all-reduce.4.cloned.1.call-done
  99.4 1.1 subtract_convert_fusion
  100.5 0.1 pad_maximum_fusion
  100.7 31.4 %all_gather.9 = bf16[2,16,8192]{2,1,0:T(8,128)(2,1)S(1)} all-gather(bf16[2,16,1024]{2,1,0:T(8,128)(2,1)S(1)} %convert_element_type.53), channel_id=1, replica_groups=mesh['ga'=2,'gy'=8,'gx'=2] {'gy'}, dimensions={2}, use_global_device_ids=true | all-gather | bytes 589824 | tf_op jit(solution)/shard_map/all_gather | solution.py:78
  132.1 1.3 fusion.37
  133.4 5.8 %fusion.8 = (f32[16,4,2,8]{3,2,1,0:T(2,128)S(1)}, f32[16,4,2,8,512]{4,3,2,1,0:T(8,128)S(1)}) fusion(pred[16,512]{1,0:T(8,128)(4,1)S(1)} %broadcast_compare_fusion, bf16[16,512,4,128,1]{3,2,1,0,4:T(4,128)(2,1)} %bitcast.41, bf16[2,16,4,8,128]{4,3,2,1,0:T(8,128)(2,1)S(1)} %bitcast.44), kind=kOutput, calls=%fused_computation.10 | convolution fusion | flops 135789568 | bytes 10760192 | tf_op jit(solution)/shard_map/cbkgd,bpkd->bkcgp/dot_general | solution.py:101
  139.3 34.5 %pmax.7 = f32[16,4,2,8]{3,2,1,0:T(2,128)S(1)} all-reduce(f32[16,4,2,8]{3,2,1,0:T(2,128)S(1)} %max.5), channel_id=1, replica_groups=mesh['ga'=2,'gy'=8,'gx'=2] {'gy'}, use_global_device_ids=true, to_apply=%region_5.6 | all-reduce | flops 1024 | bytes 8192 | tf_op jit(solution)/shard_map/pmax | solution.py:118
  173.7 5.7 %fusion.2 = f32[16,4,2,8,128]{4,3,2,1,0:T(8,128)} fusion(bf16[16,512,4,128,1]{3,2,1,0,4:T(4,128)(2,1)} %bitcast.42, f32[16,4,2,8,512]{4,3,2,1,0:T(8,128)S(1)} %get-tuple-element.17, f32[16,4,2,8]{3,2,1,0:T(2,128)S(1)} %pmax.7, pred[16,512]{1,0:T(8,128)(4,1)S(1)} %broadcast_compare_fusion), kind=kOutput, calls=%fused_computation.2 | convolution fusion | flops 136314880 | bytes 11022336 | tf_op jit(solution)/shard_map/bkcgp,bpkd->bkcgd/dot_general | solution.py:123
  179.4 0.0 all-reduce.6.cloned.1.call-update
  179.4 0.0 reduce-scatter.2.cloned.1.call-start
  179.5 0.8 fusion.9
  180.3 34.5 %psum.39 = f32[16,4,2,8]{3,2,1,0:T(2,128)S(1)} all-reduce(f32[16,4,2,8]{3,2,1,0:T(2,128)S(1)} %fusion.9), channel_id=1, replica_groups=mesh['ga'=2,'gy'=8,'gx'=2] {'gy'}, use_global_device_ids=true, to_apply=%region_9.10 | all-reduce | flops 1024 | bytes 8192 | tf_op jit(solution)/shard_map/psum | solution.py:135
  214.8 0.3 fusion.28
  215.1 34.6 %all-reduce.6.cloned.1.call-done = f32[16,4,2,8,128]{4,3,2,1,0:T(8,128)} async-done(((f32[16,4,2,8,128]{4,3,2,1,0:T(8,128)}), f32[16,4,2,8,128]{4,3,2,1,0:T(8,128)}) %all-reduce.6.cloned.1.call-update) | async-done | bytes 524304 | tf_op jit(solution)/shard_map/psum | solution.py:135
  249.7 1.4 fusion.13
  251.1 0.1 reshape.120
  251.2 5.6 %fusion = f32[2,16,1024]{2,1,0:T(8,128)} fusion(bf16[2,16,4096]{2,1,0:T(8,128)(2,1)S(1)} %reshape.120, bf16[4096,1024]{1,0:T(8,128)(2,1)} %param.14), kind=kOutput, calls=%fused_computation | convolution fusion | flops 268435456 | bytes 8781824 | tf_op jit(solution)/shard_map/yjz,zo->yjo/dot_general | solution.py:142
  256.8 0.0 reduce-scatter.2.cloned.1.call-update
  256.9 0.7 copy.40
  257.6 6.2 %reduce-scatter.2.cloned.1.call-done = f32[2,16,512]{2,1,0:T(8,128)} async-done(((f32[2,16,1024]{2,1,0:T(8,128)}), f32[2,16,512]{2,1,0:T(8,128)}) %reduce-scatter.2.cloned.1.call-update) | async-done | bytes 65552 | tf_op jit(solution)/shard_map/reduce_scatter | solution.py:145
  263.8 1.5 add_convert_fusion.1
  (24 shorter events, 0.4 us)
Async XLA Ops:
  7.2 9.0 %copy-start = (bf16[4096,128]{1,0:T(8,128)(2,1)S(1)}, bf16[4096,128]{1,0:T(8,128)(2,1)}, u32[]{:S(2)}) copy-start(bf16[4096,128]{1,0:T(8,128)(2,1)} %param.12) | copy-start | bytes 3145732
  7.2 2.5 copy-start.3
  7.2 92.2 %all-reduce.4.cloned.1.call-start = ((), (), s32[]{:S(2)}) async-start(), calls=%async_computation.1 | async-start | bytes 262144 | tf_op jit(solution)/shard_map/psum | solution.py:73
  9.7 5.3 %copy-start.1 = (f32[2,16,8192]{2,1,0:T(8,128)}, f32[2,16,8192]{2,1,0:T(8,128)S(1)}, u32[]{:S(2)}) copy-start(f32[2,16,8192]{2,1,0:T(8,128)S(1)} %convert_element_type.49) | copy-start | bytes 3145732
  9.9 5.9 %copy-start.4 = (s32[16]{0:T(128)S(1)}, s32[16]{0:T(128)}, u32[]{:S(2)}) copy-start(s32[16]{0:T(128)} %param.17) | copy-start | bytes 196
  9.9 6.5 %copy-start.2 = (bf16[4096,128]{1,0:T(8,128)(2,1)S(1)}, bf16[4096,128]{1,0:T(8,128)(2,1)}, u32[]{:S(2)}) copy-start(bf16[4096,128]{1,0:T(8,128)(2,1)} %param.13) | copy-start | bytes 3145732
  15.7 233.9 %all-reduce.6.cloned.1.call-start = ((), (), s32[]{:S(2)}) async-start(), calls=%async_computation.2 | async-start | bytes 1048576 | tf_op jit(solution)/shard_map/psum | solution.py:135
  179.4 84.3 %reduce-scatter.2.cloned.1.call-start = ((), (), s32[]{:S(2)}) async-start(), calls=%async_computation.3 | async-start | bytes 196608 | tf_op jit(solution)/shard_map/reduce_scatter | solution.py:145
Sparse Core Ops, SparseCore 0:
  15.9 20.6 all-reduce.3
  179.6 70.0 all-reduce.5
  256.9 6.7 reduce-scatter.1

commit v2 on v1

--- a/solution.py
+++ b/solution.py
@@ -1,8 +1,12 @@
+import functools
 import math
 
 import jax
 import jax.numpy as jnp
+import numpy as np
 from jax import lax
+from jax.experimental import pallas as pl
+from jax.experimental.pallas import tpu as pltpu
 from jax.sharding import PartitionSpec as P
 
 HQ = 64
@@ -147,9 +151,418 @@
     return (mixed_all, fresh_all)
 
 
+MESH = pl.DeviceIdType.MESH
+LOW = -1e30
+CHUNKS = 8
+
+
+def block_kernel(
+    n_gy,
+    len_ref, gain_ref, freq_ref, x_hbm, wq_hbm, wk_hbm, wv_hbm, wo_hbm, kc_hbm, vc_hbm,
+    mixed_ref, fresh_ref,
+    x_v, xn_v, w_v, wo_v, kc_v, vc_v, part, part_in, qsort, pack, gath, kvf,
+    acc_s, acc_r, ml_s, ml_r, fresh_acc, att, flat, lhs, po_s, po_r,
+    sem_x, sem_wq, sem_wk, sem_wv, sem_kc, sem_vc, sem_wo,
+    pair_s, pair_r, gath_s, gath_r, accs, accr, mls, mlr, atts, attr, out_s, out_r,
+):
+    gx = lax.axis_index("gx")
+    gy = lax.axis_index("gy")
+    half = w_v.shape[0]
+    qw = wq_hbm.shape[1]
+    heads = kc_hbm.shape[2] // HD
+    rows = kc_hbm.shape[0]
+    span = kc_hbm.shape[1]
+    own = rows // n_gy
+    group = HQ // KV
+    hb = rows // 2
+    combos = own * heads
+    per_gx = n_gy // 2
+    target = gy // per_gx
+    scale = HD ** (-0.5)
+    step_rows = half // CHUNKS
+
+    def owner_of(d):
+        return lax.rem(gy + 1 + d, n_gy)
+
+    copy_x = pltpu.make_async_copy(x_hbm, x_v, sem_x)
+    copy_x.start()
+
+    def wq_copies(c):
+        r = pl.ds(c * step_rows, step_rows)
+        return (
+            pltpu.make_async_copy(wq_hbm.at[r], w_v.at[r, pl.ds(0, qw)], sem_wq.at[c]),
+            pltpu.make_async_copy(wk_hbm.at[r], w_v.at[r, pl.ds(qw, HD)], sem_wk.at[c]),
+            pltpu.make_async_copy(wv_hbm.at[r], w_v.at[r, pl.ds(qw + HD, HD)], sem_wv.at[c]),
+        )
+
+    def cache_copies(d):
+        r = pl.ds(owner_of(d) * own, own)
+        return (
+            pltpu.make_async_copy(kc_hbm.at[r], kc_v.at[d], sem_kc.at[d]),
+            pltpu.make_async_copy(vc_hbm.at[r], vc_v.at[d], sem_vc.at[d]),
+        )
+
+    oc = wo_hbm.shape[1] // 2
+    ok = half // 4
+
+    def wo_copy(p, c):
+        which = (1 - gx) if p == 0 else gx
+        r = pl.ds(c * ok, ok)
+        return pltpu.make_async_copy(
+            wo_hbm.at[r, pl.ds(pl.multiple_of(which * oc, oc), oc)], wo_v.at[p, r], sem_wo.at[p * 4 + c]
+        )
+
+    for c in range(CHUNKS):
+        for copy in wq_copies(c):
+            copy.start()
+
+    barrier = pltpu.get_barrier_semaphore()
+    for d in range(1, n_gy):
+        for g in range(2):
+            pl.semaphore_signal(
+                barrier, inc=1, device_id={"gy": lax.rem(gy + d, n_gy), "gx": g}, device_id_type=MESH
+            )
+    pl.semaphore_signal(barrier, inc=1, device_id={"gx": 1 - gx}, device_id_type=MESH)
+
+    for d in range(n_gy):
+        for copy in cache_copies(d):
+            copy.start()
+    for p in range(2):
+        for c in range(4):
+            wo_copy(p, c).start()
+
+    row16 = lax.broadcasted_iota(jnp.int32, (2 * hb, HD), 0)
+    lane16 = lax.broadcasted_iota(jnp.int32, (2 * hb, HD), 1)
+    pos = jnp.zeros((2 * hb, HD), jnp.float32)
+    for r in range(hb):
+        pos = jnp.where(row16 % hb == r, len_ref[gx * hb + r].astype(jnp.float32), pos)
+    pos = pos + (row16 // hb).astype(jnp.float32)
+    angle = pos * freq_ref[...]
+    cos_t = jnp.cos(angle)
+    sin_t = jnp.sin(angle)
+    sin_t = jnp.where(lane16 < HD // 2, -sin_t, sin_t)
+
+    def rope(u):
+        return u * cos_t + pltpu.roll(u, HD // 2, 1) * sin_t
+
+    copy_x.wait()
+    width = x_v.shape[1]
+    total = jnp.zeros((x_v.shape[0], 1024), jnp.float32)
+    for c in range(width // 1024):
+        xf = x_v[:, c * 1024 : (c + 1) * 1024].astype(jnp.float32)
+        total = total + xf * xf
+    inv = lax.rsqrt(jnp.sum(total, axis=1, keepdims=True) * (1.0 / width) + EPS)
+    for c in range(half // 1024):
+        cols = pl.ds(pl.multiple_of(gx * half + c * 1024, 1024), 1024)
+        xf = x_v[:, cols].astype(jnp.float32)
+        xn_v[:, c * 1024 : (c + 1) * 1024] = (xf * inv * gain_ref[:, cols]).astype(jnp.bfloat16)
+
+    acc = jnp.zeros((x_v.shape[0], w_v.shape[1]), jnp.float32)
+    for c in range(CHUNKS):
+        for copy in wq_copies(c):
+            copy.wait()
+        r = slice(c * step_rows, (c + 1) * step_rows)
+        acc = acc + jnp.dot(xn_v[:, r], w_v[r, :], preferred_element_type=jnp.float32)
+    for c in range(2):
+        for s in range(2):
+            part[c, s * hb : (s + 1) * hb, :] = acc[s * rows + c * hb : s * rows + (c + 1) * hb]
+
+    pl.semaphore_wait(barrier, 2 * n_gy - 1)
+    pair = pltpu.make_async_remote_copy(
+        src_ref=part.at[1 - gx], dst_ref=part_in, send_sem=pair_s, recv_sem=pair_r,
+        device_id={"gx": 1 - gx}, device_id_type=MESH,
+    )
+    pair.start()
+    pair.wait_recv()
+    tot = part[gx] + part_in[...]
+    for g in range(group):
+        u = rope(tot[:, g * HD : (g + 1) * HD])
+        for s in range(2):
+            qsort[pl.ds(s * group + g, hb, stride=2 * group), :] = u[s * hb : (s + 1) * hb]
+    nq = hb * 2 * group
+    pack[0:nq, :] = qsort[...].astype(jnp.bfloat16)
+    kraw = tot[:, qw : qw + HD].astype(jnp.bfloat16).astype(jnp.float32)
+    pack[nq : nq + 2 * hb, :] = rope(kraw).astype(jnp.bfloat16)
+    pack[nq + 2 * hb : nq + 4 * hb, :] = tot[:, qw + HD : qw + 2 * HD].astype(jnp.bfloat16)
+
+    slot = lax.rem(gy, per_gx) * 2 + gx
+    here = target == gx
+
+    def gather_copy(i, at):
+        return pltpu.make_async_remote_copy(
+            src_ref=pack, dst_ref=gath.at[at], send_sem=gath_s.at[i], recv_sem=gath_r.at[at],
+            device_id={"gy": lax.rem(gy + i, n_gy), "gx": target}, device_id_type=MESH,
+        )
+
+    for i in range(1, n_gy):
+        gather_copy(i, slot).start()
+
+    @pl.when(here)
+    def _():
+        gath[slot] = pack[...]
+
+    @pl.when(jnp.logical_not(here))
+    def _():
+        gather_copy(0, slot).start()
+
+    for k in range(2 * per_gx):
+        mine = jnp.logical_and(here, slot == k)
+
+        @pl.when(jnp.logical_not(mine))
+        def _():
+            gather_copy(1, k).wait_recv()
+
+    lane_ml = lax.broadcasted_iota(jnp.int32, (2 * group, HD), 1)
+    lane_s = lax.broadcasted_iota(jnp.int32, (2 * group, span), 1) + gy * span
+
+    def send_acc(d):
+        return pltpu.make_async_remote_copy(
+            src_ref=acc_s.at[d], dst_ref=acc_r.at[d], send_sem=accs.at[d], recv_sem=accr.at[d],
+            device_id={"gy": owner_of(d)}, device_id_type=MESH,
+        )
+
+    def send_ml(d):
+        return pltpu.make_async_remote_copy(
+            src_ref=ml_s.at[d], dst_ref=ml_r.at[d], send_sem=mls.at[d], recv_sem=mlr.at[d],
+            device_id={"gy": owner_of(d)}, device_id_type=MESH,
+        )
+
+    nqr = 2 * group
+
+    def attend(d, carry):
+        for copy in cache_copies(d):
+            copy.wait()
+        owner = owner_of(d)
+        ml = jnp.zeros((nqr, HD), jnp.float32)
+        for i in range(own):
+            b = owner * own + i
+            c = b // hb
+            bl = lax.rem(b, hb)
+            seen = lane_s < len_ref[b]
+            for h in range(heads):
+                k = i * heads + h
+                q = gath[h * 2 + c, pl.ds(pl.multiple_of(bl * nqr, nqr), nqr), :]
+                score = lax.dot_general(
+                    q, kc_v[d, i, :, h * HD : (h + 1) * HD], (((1,), (1,)), ((), ())),
+                    preferred_element_type=jnp.float32,
+                ) * scale
+                score = jnp.where(seen, score, LOW)
+                m = jnp.max(score, axis=1, keepdims=True)
+                p = jnp.where(seen, jnp.exp(score - m), 0.0)
+                o = jnp.dot(
+                    p.astype(jnp.bfloat16), vc_v[d, i, :, h * HD : (h + 1) * HD],
+                    preferred_element_type=jnp.float32,
+                )
+                acc_s[d, k * nqr : (k + 1) * nqr, :] = o.astype(jnp.bfloat16)
+                ml = jnp.where(lane_ml == k, m, ml)
+                ml = jnp.where(lane_ml == k + HD // 2, jnp.sum(p, axis=1, keepdims=True), ml)
+        ml_s[d] = ml
+
+        @pl.when(d < n_gy - 1)
+        def _():
+            send_acc(d).start()
+            send_ml(d).start()
+
+        return carry
+
+    lax.fori_loop(0, n_gy, attend, 0)
+
+    for k in range(2 * heads):
+        kvf[k] = gath[k, nq : nq + 4 * hb, :].astype(jnp.float32)
+    for s in range(2):
+        for t in range(2):
+            for h in range(heads):
+                at = t * 2 * hb + s * hb
+                fresh_ref[s * rows : (s + 1) * rows, (t * heads + h) * HD : (t * heads + h + 1) * HD] = (
+                    jnp.concatenate([kvf[2 * h, at : at + hb, :], kvf[2 * h + 1, at : at + hb, :]], axis=0)
+                ).astype(jnp.bfloat16)
+
+    later = lax.broadcasted_iota(jnp.int32, (nqr, 1), 0) >= group
+    mlf = jnp.zeros((nqr, HD), jnp.float32)
+    for i in range(own):
+        b = gy * own + i
+        c = b // hb
+        bl = lax.rem(b, hb)
+        for h in range(heads):
+            k = i * heads + h
+            q = gath[h * 2 + c, pl.ds(pl.multiple_of(bl * nqr, nqr), nqr), :].astype(jnp.float32)
+            f = []
+            for s in range(2):
+                key = kvf[h * 2 + c, pl.ds(s * hb + bl, 1), :]
+                f.append(jnp.sum(q * key, axis=1, keepdims=True) * scale)
+            f[1] = jnp.where(later, f[1], LOW)
+            m = jnp.maximum(f[0], f[1])
+            p0 = jnp.exp(f[0] - m)
+            p1 = jnp.where(later, jnp.exp(f[1] - m), 0.0)
+            v0 = kvf[h * 2 + c, pl.ds(2 * hb + bl, 1), :]
+            v1 = kvf[h * 2 + c, pl.ds(3 * hb + bl, 1), :]
+            fresh_acc[k * nqr : (k + 1) * nqr, :] = (
+                p0.astype(jnp.bfloat16).astype(jnp.float32) * v0
+                + p1.astype(jnp.bfloat16).astype(jnp.float32) * v1
+            )
+            mlf = jnp.where(lane_ml == k, m, mlf)
+            mlf = jnp.where(lane_ml == k + HD // 2, p0 + p1, mlf)
+
+    for d in range(n_gy - 1):
+        send_ml(d).wait_recv()
+    ml_all = [ml_r[d] for d in range(n_gy - 1)] + [ml_s[n_gy - 1], mlf]
+    peak = ml_all[0]
+    for ml in ml_all[1:]:
+        peak = jnp.maximum(peak, ml)
+    factors = [jnp.exp(ml - peak) for ml in ml_all]
+    weight = jnp.zeros_like(peak)
+    for f, ml in zip(factors, ml_all):
+        weight = weight + f * pltpu.roll(ml, HD // 2, 1)
+    for d in range(n_gy - 1):
+        send_acc(d).wait_recv()
+    for k in range(combos):
+        r = slice(k * nqr, (k + 1) * nqr)
+        o = factors[n_gy][:, k : k + 1] * fresh_acc[r, :]
+        for d in range(n_gy):
+            a = acc_r[d, r, :] if d < n_gy - 1 else acc_s[d, r, :]
+            o = o + factors[d][:, k : k + 1] * a.astype(jnp.float32)
+        att[gy, r, :] = (o / weight[:, k : k + 1]).astype(jnp.bfloat16)
+
+    def att_copy(d, at):
+        return pltpu.make_async_remote_copy(
+            src_ref=att.at[at], dst_ref=att.at[at], send_sem=atts.at[d - 1], recv_sem=attr.at[at],
+            device_id={"gy": lax.rem(gy + d, n_gy)}, device_id_type=MESH,
+        )
+
+    for d in range(1, n_gy):
+        att_copy(d, gy).start()
+    for d in range(1, n_gy):
+        att_copy(d, lax.rem(gy + d, n_gy)).wait_recv()
+    size = combos * nqr
+    for j in range(n_gy):
+        flat[j * size : (j + 1) * size, :] = att[j].astype(jnp.float32)
+    for h in range(heads):
+        for g in range(group):
+            for s in range(2):
+                lhs[s * rows : (s + 1) * rows, (h * group + g) * HD : (h * group + g + 1) * HD] = flat[
+                    pl.ds(h * nqr + s * group + g, rows, stride=heads * nqr), :
+                ].astype(jnp.bfloat16)
+
+    def project(p):
+        total = jnp.zeros((2 * rows, oc), jnp.float32)
+        for c in range(4):
+            wo_copy(p, c).wait()
+            r = slice(c * ok, (c + 1) * ok)
+            total = total + jnp.dot(lhs[:, r], wo_v[p, r, :], preferred_element_type=jnp.float32)
+        return total
+
+    po_s[...] = project(0)
+    out_copy = pltpu.make_async_remote_copy(
+        src_ref=po_s, dst_ref=po_r, send_sem=out_s, recv_sem=out_r,
+        device_id={"gx": 1 - gx}, device_id_type=MESH,
+    )
+    out_copy.start()
+    mine_out = project(1)
+    residual = x_v[:, pl.ds(pl.multiple_of((gy * 2 + gx) * oc, oc), oc)].astype(jnp.float32)
+    out_copy.wait_recv()
+    mixed_ref[...] = (residual + (mine_out + po_r[...])).astype(jnp.bfloat16)
+
+    pair.wait_send()
+    for i in range(1, n_gy):
+        gather_copy(i, slot).wait_send()
+
+    @pl.when(jnp.logical_not(here))
+    def _():
+        gather_copy(0, slot).wait_send()
+
+    for d in range(n_gy - 1):
+        send_acc(d).wait_send()
+        send_ml(d).wait_send()
+    for d in range(1, n_gy):
+        att_copy(d, gy).wait_send()
+    out_copy.wait_send()
+
+
+def on_device_kernel(
+    inputs, norm_gain, w_query, w_key, w_value, output_weight, cache_keys, cache_values, lengths
+):
+    n_gy = lax.axis_size("gy")
+    steps, rows, width = inputs.shape
+    half, qw = w_query.shape
+    span, kvl = cache_keys.shape[1:]
+    heads = kvl // HD
+    own = rows // n_gy
+    group = HQ // KV
+    nqr = 2 * group
+    hb = rows // 2
+    size = own * heads * nqr
+    oc = output_weight.shape[1] // 2
+    npack = hb * nqr + 4 * hb
+    freq = np.exp(np.arange(HD // 2) * (-2.0 * math.log(THETA) / HD))
+    freq = jnp.asarray(np.tile(freq, 2)[None, :], jnp.float32)
+    f32, b16 = jnp.float32, jnp.bfloat16
+    dma = pltpu.SemaphoreType.DMA
+    vmem = pl.BlockSpec(memory_space=pltpu.VMEM)
+    hbm = pl.BlockSpec(memory_space=pl.ANY)
+    mixed, fresh = pl.pallas_call(
+        functools.partial(block_kernel, n_gy),
+        out_shape=(
+            jax.ShapeDtypeStruct((steps * rows, oc), b16),
+            jax.ShapeDtypeStruct((steps * rows, 2 * kvl), b16),
+        ),
+        in_specs=[pl.BlockSpec(memory_space=pltpu.SMEM), vmem, vmem] + [hbm] * 7,
+        out_specs=(vmem, vmem),
+        scratch_shapes=[
+            pltpu.VMEM((steps * rows, width), b16),
+            pltpu.VMEM((steps * rows, half), b16),
+            pltpu.VMEM((half, qw + 2 * HD), b16),
+            pltpu.VMEM((2, half, oc), b16),
+            pltpu.VMEM((n_gy, own, span, kvl), b16),
+            pltpu.VMEM((n_gy, own, span, kvl), b16),
+            pltpu.VMEM((2, steps * hb, qw + 2 * HD), f32),
+            pltpu.VMEM((steps * hb, qw + 2 * HD), f32),
+            pltpu.VMEM((hb * nqr, HD), f32),
+            pltpu.VMEM((npack, HD), b16),
+            pltpu.VMEM((2 * heads, npack, HD), b16),
+            pltpu.VMEM((2 * heads, 4 * hb, HD), f32),
+            pltpu.VMEM((n_gy, size, HD), b16),
+            pltpu.VMEM((n_gy - 1, size, HD), b16),
+            pltpu.VMEM((n_gy, nqr, HD), f32),
+            pltpu.VMEM((n_gy - 1, nqr, HD), f32),
+            pltpu.VMEM((size, HD), f32),
+            pltpu.VMEM((n_gy, size, HD), b16),
+            pltpu.VMEM((n_gy * size, HD), f32),
+            pltpu.VMEM((steps * rows, half), b16),
+            pltpu.VMEM((steps * rows, oc), f32),
+            pltpu.VMEM((steps * rows, oc), f32),
+            dma, dma((CHUNKS,)), dma((CHUNKS,)), dma((CHUNKS,)), dma((n_gy,)), dma((n_gy,)), dma((8,)),
+            dma, dma, dma((n_gy,)), dma((2 * heads,)),
+            dma((n_gy - 1,)), dma((n_gy - 1,)), dma((n_gy - 1,)), dma((n_gy - 1,)),
+            dma((n_gy - 1,)), dma((n_gy,)), dma, dma,
+        ],
+        compiler_params=pltpu.CompilerParams(
+            collective_id=0, has_side_effects=True, vmem_limit_bytes=52 * 1024 * 1024
+        ),
+        name="decode_block",
+    )(
+        lengths, norm_gain.astype(f32).reshape(1, width), freq, inputs.reshape(steps * rows, width),
+        w_query, w_key, w_value, output_weight, cache_keys, cache_values,
+    )
+    return mixed.reshape(steps, rows, oc), fresh.reshape(steps, rows, 2, kvl)
+
+
+def on_device(*args):
+    inputs, _, w_query, w_key, _, output_weight, cache_keys, _, _ = args
+    n_gy, n_gx = lax.axis_size("gy"), lax.axis_size("gx")
+    fits = (
+        n_gx == 2
+        and inputs.shape[0] == 2
+        and inputs.shape[1] == 16
+        and n_gy == KV
+        and w_key.shape[1] == HD
+        and cache_keys.shape[1] % 128 == 0
+    )
+    return on_device_kernel(*args) if fits else on_device_plain(*args)
+
+
 def solution(mesh):
     return jax.shard_map(
-        on_device_plain,
+        on_device,
         mesh=mesh,
         in_specs=(
             P(None, "ga", None),

time: 273 us -> 50.1 us (0.18)
  blocking collectives: 158 us -> 0 us
  Pallas kernels: 0 us -> 43.6 us
  waiting for transfers between devices: 40.8 us -> 0 us
  matrix products: 25.4 us -> 0 us
  local copies, waits for them, and re-layouts: 26.9 us -> 4.85 us
  between operations: 14.1 us -> 0.64 us
  other arithmetic: 6.87 us -> 0.72 us
    all_gather x3 -> x0, blocking collectives: 84.9 us -> none  [on_device_plain(): gather = lambda a: lax.all_gather(a, 'gy', axis=2, tiled=True)]
    pallas_call x0 -> x1, Pallas kernels: none -> 43.6 us  [on_device_kernel(): pl.pallas_call(functools.partial(block_kernel, n_gy), out_shape=(jax.Shap...]
    psum x2 -> x0, blocking collectives: 38.2 us -> none  [the longest x1 34.5 us: on_device_plain(): acc_sum, total_sum = lax.psum((cache_acc, cache_total), 'gy')]
    psum x2 -> x0, waiting for transfers between devices: 34.6 us -> none  [the longest x1 34.6 us: on_device_plain(): acc_sum, total_sum = lax.psum((cache_acc, cache_total), 'gy')]
    pmax x1 -> x0, blocking collectives: 34.5 us -> none  [on_device_plain(): peak_score = lax.pmax(local_peak, 'gy')]
    dot_general x8 -> x0, matrix products: 25.4 us -> none  [the longest x1 5.78 us: on_device_plain(): jnp.einsum('cbkgd,bpkd->bkcgp', queries, keys_here, preferred_element_typ...]
    reshape x5 -> x1, local copies, waits for them, and re-layouts: 25.2 us -> 0.66 us  [on_device_kernel(): return (mixed.reshape(steps, rows, oc), fresh.reshape(steps, rows, 2, kvl))]
    reduce_scatter x1 -> x0, waiting for transfers between devices: 6.18 us -> none  [on_device_plain(): lax.psum_scatter(output_piece, 'gx', scatter_dimension=2, tiled=True)]
  transfers between devices with their start and end apart: 3 -> 0, of which waited for: 2 -> 0; matrix products, arithmetic and copies ran while one was open for 10% -> 0% of each run, Pallas kernels for 0% -> 0%
where the time goes in v2:
time: 50.1 us; the launch traced here: 49.8 us
  Pallas kernels  43.6 us (87%)
  local copies, waits for them, and re-layouts  4.85 us (10%)
  other arithmetic  0.72 us (1%)
  between operations  0.64 us (1%)
    pallas_call x1, Pallas kernels, on_device_kernel(): pl.pallas_call(functools.partial(block_kernel, n_gy), out_shape=(jax.Shap...  43.6 us
    unnamed x9, local copies, waits for them, and re-layouts  4.19 us

profile of v2, /device:TPU:0, one launch (start us, length us, event | category | flops | bytes accessed | tf_op | source)
XLA Modules:
  0.0 49.8 jit_solution(74344292625745039)
XLA Ops:
  0.6 0.7 %reshape.23 = f32[8192]{0:T(1024)S(1)} convert(bf16[8192]{0:T(1024)(128)(2,1)} %param.11) | non-fusion elementwise | flops 8192 | bytes 49152 | tf_op jit(solution)/shard_map/reshape | solution.py:543
  1.4 0.0 copy-start
  1.4 1.2 %copy-done = bf16[4096,128]{1,0:T(8,128)(2,1)S(1)} copy-done((bf16[4096,128]{1,0:T(8,128)(2,1)S(1)}, bf16[4096,128]{1,0:T(8,128)(2,1)}, u32[]{:S(2)}) %copy-start) | copy-done | bytes 1048600
  2.6 0.0 copy-start.1
  2.6 1.0 %copy-done.1 = bf16[2,16,8192]{2,1,0:T(8,128)(2,1)S(1)} copy-done((bf16[2,16,8192]{2,1,0:T(8,128)(2,1)S(1)}, bf16[2,16,8192]{2,1,0:T(8,128)(2,1)}, u32[]{:S(2)}) %copy-start.1) | copy-done | bytes 524312
  3.6 0.0 copy-start.2
  3.6 0.7 %copy-done.2 = s32[16]{0:T(128)S(1)} copy-done((s32[16]{0:T(128)S(1)}, s32[16]{0:T(128)}, u32[]{:S(2)}) %copy-start.2) | copy-done | bytes 88
  4.3 0.0 copy-start.3
  4.3 0.7 %copy-done.3 = f32[1,128]{1,0:T(1,128)S(1)} copy-done((f32[1,128]{1,0:T(1,128)S(1)}, f32[1,128]{1,0:T(1,128)}, u32[]{:S(2)}) %copy-start.3) | copy-done | bytes 536
  4.9 43.6 %decode_block.1 = (bf16[32,512]{1,0:T(8,128)(2,1)S(1)}, bf16[32,1024]{1,0:T(8,128)(2,1)S(1)}) custom-call(s32[16]{0:T(128)S(1)} %copy-done.2, f32[1,8192]{1,0:T(1,128)S(1)} %bitcast.4, f32[1,128]{1,0:T(1,128)S(1)} %copy-done.3, bf16[32,8192]{1,0:T(8,128)(2,1)S(1)} %bitcast.3, bf16[4096,1024]{1,0:T(8,128)(2,1)} %wq_hbm.1, bf16[4096,128]{1,0:T(8,128)(2,1)S(1)} %copy-done, ...), custom_call_target="tpu_custom_call" | custom-call | tf_op jit(solution)/shard_map/decode_block/pallas_call | solution.py:502
  48.5 0.7 %reshape.22 = bf16[2,16,2,512]{3,2,1,0:T(2,128)(2,1)} reshape(bf16[32,1024]{1,0:T(8,128)(2,1)S(1)} %get-tuple-element.5) | data formatting | bytes 131072 | tf_op jit(solution)/shard_map/reshape | solution.py:546
  49.2 0.6 %copy.13 = bf16[2,16,512]{2,1,0:T(8,128)(2,1)} copy(bf16[2,16,512]{2,1,0:T(8,128)(2,1)S(1)} %bitcast.5) | data formatting | bytes 65536
Async XLA Ops:
  1.4 1.2 %copy-start = (bf16[4096,128]{1,0:T(8,128)(2,1)S(1)}, bf16[4096,128]{1,0:T(8,128)(2,1)}, u32[]{:S(2)}) copy-start(bf16[4096,128]{1,0:T(8,128)(2,1)} %wk_hbm.1) | copy-start | bytes 3145732
  2.6 1.0 %copy-start.1 = (bf16[2,16,8192]{2,1,0:T(8,128)(2,1)S(1)}, bf16[2,16,8192]{2,1,0:T(8,128)(2,1)}, u32[]{:S(2)}) copy-start(bf16[2,16,8192]{2,1,0:T(8,128)(2,1)} %param.10) | copy-start | bytes 1572868
  3.6 0.7 %copy-start.2 = (s32[16]{0:T(128)S(1)}, s32[16]{0:T(128)}, u32[]{:S(2)}) copy-start(s32[16]{0:T(128)} %len_ref.1) | copy-start | bytes 196
  4.3 0.7 %copy-start.3 = (f32[1,128]{1,0:T(1,128)S(1)}, f32[1,128]{1,0:T(1,128)}, u32[]{:S(2)}) copy-start(f32[1,128]{1,0:T(1,128)} %constant.2.clone.freq_ref) | copy-start | bytes 1540

commit v3 on v2

--- a/solution.py
+++ b/solution.py
@@ -154,16 +154,18 @@
 MESH = pl.DeviceIdType.MESH
 LOW = -1e30
 CHUNKS = 8
+VMEM_BYTES = 64 * 1024 * 1024
 
 
 def block_kernel(
     n_gy,
-    len_ref, gain_ref, freq_ref, x_hbm, wq_hbm, wk_hbm, wv_hbm, wo_hbm, kc_hbm, vc_hbm,
+    len_hbm, gain_ref, freq_hbm, x_hbm, wq_hbm, wk_hbm, wv_hbm, wo_hbm, kc_hbm, vc_hbm,
     mixed_ref, fresh_ref,
+    len_ref, freq_ref,
     x_v, xn_v, w_v, wo_v, kc_v, vc_v, part, part_in, qsort, pack, gath, kvf,
     acc_s, acc_r, ml_s, ml_r, fresh_acc, att, flat, lhs, po_s, po_r,
-    sem_x, sem_wq, sem_wk, sem_wv, sem_kc, sem_vc, sem_wo,
-    pair_s, pair_r, gath_s, gath_r, accs, accr, mls, mlr, atts, attr, out_s, out_r,
+    sem_len, sem_freq, sem_x, sem_wq, sem_wk, sem_wv, sem_kc, sem_vc, sem_wo,
+    pair_s, pair_r, gath_s, gath_r, fwd_s, accs, accr, mls, mlr, atts, attr, out_s, out_r,
 ):
     gx = lax.axis_index("gx")
     gy = lax.axis_index("gy")
@@ -186,6 +188,10 @@
 
     copy_x = pltpu.make_async_copy(x_hbm, x_v, sem_x)
     copy_x.start()
+    copy_len = pltpu.make_async_copy(len_hbm, len_ref, sem_len)
+    copy_len.start()
+    copy_freq = pltpu.make_async_copy(freq_hbm, freq_ref, sem_freq)
+    copy_freq.start()
 
     def wq_copies(c):
         r = pl.ds(c * step_rows, step_rows)
@@ -224,12 +230,8 @@
             )
     pl.semaphore_signal(barrier, inc=1, device_id={"gx": 1 - gx}, device_id_type=MESH)
 
-    for d in range(n_gy):
-        for copy in cache_copies(d):
-            copy.start()
-    for p in range(2):
-        for c in range(4):
-            wo_copy(p, c).start()
+    copy_len.wait()
+    copy_freq.wait()
 
     row16 = lax.broadcasted_iota(jnp.int32, (2 * hb, HD), 0)
     lane16 = lax.broadcasted_iota(jnp.int32, (2 * hb, HD), 1)
@@ -261,6 +263,10 @@
     for c in range(CHUNKS):
         for copy in wq_copies(c):
             copy.wait()
+        if c >= CHUNKS - 4:
+            for d in range(2 * (c - CHUNKS + 4), 2 * (c - CHUNKS + 5)):
+                for copy in cache_copies(d):
+                    copy.start()
         r = slice(c * step_rows, (c + 1) * step_rows)
         acc = acc + jnp.dot(xn_v[:, r], w_v[r, :], preferred_element_type=jnp.float32)
     for c in range(2):
@@ -274,6 +280,9 @@
     )
     pair.start()
     pair.wait_recv()
+    for p in range(2):
+        for c in range(4):
+            wo_copy(p, c).start()
     tot = part[gx] + part_in[...]
     for g in range(group):
         u = rope(tot[:, g * HD : (g + 1) * HD])
@@ -291,10 +300,10 @@
     def gather_copy(i, at):
         return pltpu.make_async_remote_copy(
             src_ref=pack, dst_ref=gath.at[at], send_sem=gath_s.at[i], recv_sem=gath_r.at[at],
-            device_id={"gy": lax.rem(gy + i, n_gy), "gx": target}, device_id_type=MESH,
-        )
-
-    for i in range(1, n_gy):
+            device_id={"gy": lax.rem(gy + 2 * i, n_gy), "gx": target}, device_id_type=MESH,
+        )
+
+    for i in range(1, n_gy // 2):
         gather_copy(i, slot).start()
 
     @pl.when(here)
@@ -305,12 +314,27 @@
     def _():
         gather_copy(0, slot).start()
 
-    for k in range(2 * per_gx):
-        mine = jnp.logical_and(here, slot == k)
+    odd = lax.rem(gy, 2)
+    across = gy + 1 - 2 * odd
+
+    def forward(j):
+        at = (j // 2) * 4 + odd * 2 + j % 2
+        return at, pltpu.make_async_remote_copy(
+            src_ref=gath.at[at], dst_ref=gath.at[at], send_sem=fwd_s.at[j], recv_sem=gath_r.at[at],
+            device_id={"gy": across}, device_id_type=MESH,
+        )
+
+    for j in range(heads):
+        at, onward = forward(j)
+        mine = jnp.logical_and(here, slot == at)
 
         @pl.when(jnp.logical_not(mine))
         def _():
-            gather_copy(1, k).wait_recv()
+            gather_copy(1, at).wait_recv()
+
+        onward.start()
+    for j in range(heads):
+        gather_copy(1, (j // 2) * 4 + (1 - odd) * 2 + j % 2).wait_recv()
 
     lane_ml = lax.broadcasted_iota(jnp.int32, (2 * group, HD), 1)
     lane_s = lax.broadcasted_iota(jnp.int32, (2 * group, span), 1) + gy * span
@@ -334,28 +358,33 @@
             copy.wait()
         owner = owner_of(d)
         ml = jnp.zeros((nqr, HD), jnp.float32)
-        for i in range(own):
-            b = owner * own + i
-            c = b // hb
-            bl = lax.rem(b, hb)
-            seen = lane_s < len_ref[b]
-            for h in range(heads):
-                k = i * heads + h
-                q = gath[h * 2 + c, pl.ds(pl.multiple_of(bl * nqr, nqr), nqr), :]
-                score = lax.dot_general(
-                    q, kc_v[d, i, :, h * HD : (h + 1) * HD], (((1,), (1,)), ((), ())),
-                    preferred_element_type=jnp.float32,
-                ) * scale
-                score = jnp.where(seen, score, LOW)
-                m = jnp.max(score, axis=1, keepdims=True)
-                p = jnp.where(seen, jnp.exp(score - m), 0.0)
-                o = jnp.dot(
-                    p.astype(jnp.bfloat16), vc_v[d, i, :, h * HD : (h + 1) * HD],
-                    preferred_element_type=jnp.float32,
-                )
-                acc_s[d, k * nqr : (k + 1) * nqr, :] = o.astype(jnp.bfloat16)
-                ml = jnp.where(lane_ml == k, m, ml)
-                ml = jnp.where(lane_ml == k + HD // 2, jnp.sum(p, axis=1, keepdims=True), ml)
+        ks = [(i, h) for i in range(own) for h in range(heads)]
+        rows_b = [owner * own + i for i in range(own)]
+        seen = [lane_s < len_ref[b] for b in rows_b]
+        scores = [
+            lax.dot_general(
+                gath[h * 2 + rows_b[i] // hb,
+                     pl.ds(pl.multiple_of(lax.rem(rows_b[i], hb) * nqr, nqr), nqr), :],
+                kc_v[d, i, :, h * HD : (h + 1) * HD], (((1,), (1,)), ((), ())),
+                preferred_element_type=jnp.float32,
+            )
+            for i, h in ks
+        ]
+        scores = [jnp.where(seen[i], s * scale, LOW) for (i, h), s in zip(ks, scores)]
+        peaks = [jnp.max(s, axis=1, keepdims=True) for s in scores]
+        probs = [jnp.where(seen[i], jnp.exp(s - m), 0.0) for (i, h), s, m in zip(ks, scores, peaks)]
+        outs = [
+            jnp.dot(
+                p.astype(jnp.bfloat16), vc_v[d, i, :, h * HD : (h + 1) * HD],
+                preferred_element_type=jnp.float32,
+            )
+            for (i, h), p in zip(ks, probs)
+        ]
+        sums = [jnp.sum(p, axis=1, keepdims=True) for p in probs]
+        for k in range(combos):
+            acc_s[d, k * nqr : (k + 1) * nqr, :] = outs[k].astype(jnp.bfloat16)
+            ml = jnp.where(lane_ml == k, peaks[k], ml)
+            ml = jnp.where(lane_ml == k + HD // 2, sums[k], ml)
         ml_s[d] = ml
 
         @pl.when(d < n_gy - 1)
@@ -423,16 +452,25 @@
             o = o + factors[d][:, k : k + 1] * a.astype(jnp.float32)
         att[gy, r, :] = (o / weight[:, k : k + 1]).astype(jnp.bfloat16)
 
-    def att_copy(d, at):
+    def att_copy(n, to, at):
         return pltpu.make_async_remote_copy(
-            src_ref=att.at[at], dst_ref=att.at[at], send_sem=atts.at[d - 1], recv_sem=attr.at[at],
-            device_id={"gy": lax.rem(gy + d, n_gy)}, device_id_type=MESH,
-        )
-
-    for d in range(1, n_gy):
-        att_copy(d, gy).start()
-    for d in range(1, n_gy):
-        att_copy(d, lax.rem(gy + d, n_gy)).wait_recv()
+            src_ref=att.at[at], dst_ref=att.at[at], send_sem=atts.at[n], recv_sem=attr.at[at],
+            device_id={"gy": to}, device_id_type=MESH,
+        )
+
+    side = n_gy // 2
+    sends = [att_copy(i - 1, lax.rem(gy + 2 * i, n_gy), gy) for i in range(1, side)]
+    sends.append(att_copy(side - 1, across, gy))
+    for copy in sends:
+        copy.start()
+    for i in range(1, side):
+        at = lax.rem(gy + 2 * i, n_gy)
+        onward = att_copy(side - 1 + i, across, at)
+        onward.wait_recv()
+        onward.start()
+        sends.append(onward)
+    for i in range(side):
+        att_copy(0, across, lax.rem(across + 2 * i, n_gy)).wait_recv()
     size = combos * nqr
     for j in range(n_gy):
         flat[j * size : (j + 1) * size, :] = att[j].astype(jnp.float32)
@@ -463,8 +501,10 @@
     mixed_ref[...] = (residual + (mine_out + po_r[...])).astype(jnp.bfloat16)
 
     pair.wait_send()
-    for i in range(1, n_gy):
+    for i in range(1, n_gy // 2):
         gather_copy(i, slot).wait_send()
+    for j in range(heads):
+        forward(j)[1].wait_send()
 
     @pl.when(jnp.logical_not(here))
     def _():
@@ -473,8 +513,8 @@
     for d in range(n_gy - 1):
         send_acc(d).wait_send()
         send_ml(d).wait_send()
-    for d in range(1, n_gy):
-        att_copy(d, gy).wait_send()
+    for copy in sends:
+        copy.wait_send()
     out_copy.wait_send()
 
 
@@ -498,16 +538,18 @@
     f32, b16 = jnp.float32, jnp.bfloat16
     dma = pltpu.SemaphoreType.DMA
     vmem = pl.BlockSpec(memory_space=pltpu.VMEM)
-    hbm = pl.BlockSpec(memory_space=pl.ANY)
+    hbm = pl.BlockSpec(memory_space=pltpu.HBM)
     mixed, fresh = pl.pallas_call(
         functools.partial(block_kernel, n_gy),
         out_shape=(
             jax.ShapeDtypeStruct((steps * rows, oc), b16),
             jax.ShapeDtypeStruct((steps * rows, 2 * kvl), b16),
         ),
-        in_specs=[pl.BlockSpec(memory_space=pltpu.SMEM), vmem, vmem] + [hbm] * 7,
+        in_specs=[hbm, vmem] + [hbm] * 8,
         out_specs=(vmem, vmem),
         scratch_shapes=[
+            pltpu.SMEM((rows,), jnp.int32),
+            pltpu.VMEM((1, HD), f32),
             pltpu.VMEM((steps * rows, width), b16),
             pltpu.VMEM((steps * rows, half), b16),
             pltpu.VMEM((half, qw + 2 * HD), b16),
@@ -530,13 +572,13 @@
             pltpu.VMEM((steps * rows, half), b16),
             pltpu.VMEM((steps * rows, oc), f32),
             pltpu.VMEM((steps * rows, oc), f32),
-            dma, dma((CHUNKS,)), dma((CHUNKS,)), dma((CHUNKS,)), dma((n_gy,)), dma((n_gy,)), dma((8,)),
-            dma, dma, dma((n_gy,)), dma((2 * heads,)),
+            dma, dma, dma, dma((CHUNKS,)), dma((CHUNKS,)), dma((CHUNKS,)), dma((n_gy,)), dma((n_gy,)), dma((8,)),
+            dma, dma, dma((n_gy // 2,)), dma((2 * heads,)), dma((heads,)),
             dma((n_gy - 1,)), dma((n_gy - 1,)), dma((n_gy - 1,)), dma((n_gy - 1,)),
             dma((n_gy - 1,)), dma((n_gy,)), dma, dma,
         ],
         compiler_params=pltpu.CompilerParams(
-            collective_id=0, has_side_effects=True, vmem_limit_bytes=52 * 1024 * 1024
+            collective_id=0, has_side_effects=True, vmem_limit_bytes=VMEM_BYTES
         ),
         name="decode_block",
     )(

time: 50.1 us -> 46.2 us (0.922)
  Pallas kernels: 43.6 us -> 41 us
  local copies, waits for them, and re-layouts: 4.85 us -> 2.87 us
  other arithmetic: 0.72 us -> 1.34 us
    unnamed x9 -> x1, local copies, waits for them, and re-layouts: 4.19 us -> 1.37 us
    pallas_call x1, Pallas kernels: 43.6 us -> 41 us  [on_device_kernel(): pl.pallas_call(functools.partial(block_kernel, n_gy), out_shape=(jax.Shap...]
    reshape x1, local copies, waits for them, and re-layouts: 0.66 us -> 1.5 us  [on_device_kernel(): return (mixed.reshape(steps, rows, oc), fresh.reshape(steps, rows, 2, kvl))]
    reshape x1, other arithmetic: 0.72 us -> 1.34 us  [on_device_kernel(): norm_gain.astype(f32).reshape(1, width)]
where the time goes in v3:
time: 46.2 us; the launch traced here: 45.9 us
  Pallas kernels  41 us (89%)
  local copies, waits for them, and re-layouts  2.87 us (6%)
  other arithmetic  1.34 us (3%)
  between operations  0.64 us (1%)
    pallas_call x1, Pallas kernels, on_device_kernel(): pl.pallas_call(functools.partial(block_kernel, n_gy), out_shape=(jax.Shap...  41 us
    reshape x1, local copies, waits for them, and re-layouts, on_device_kernel(): return (mixed.reshape(steps, rows, oc), fresh.reshape(steps, rows, 2, kvl))  1.5 us
    unnamed x1, local copies, waits for them, and re-layouts  1.37 us
    reshape x1, other arithmetic, on_device_kernel(): norm_gain.astype(f32).reshape(1, width)  1.34 us

profile of v3, /device:TPU:0, one launch (start us, length us, event | category | flops | bytes accessed | tf_op | source)
XLA Modules:
  0.0 45.9 jit_solution(2786449188980452197)
XLA Ops:
  0.6 1.3 %reshape.23 = f32[8192]{0:T(1024)} convert(bf16[8192]{0:T(1024)(128)(2,1)} %param.11) | non-fusion elementwise | flops 8192 | bytes 49152 | tf_op jit(solution)/shard_map/reshape | solution.py:585
  2.0 41.0 %decode_block.1 = (bf16[32,512]{1,0:T(8,128)(2,1)}, bf16[32,1024]{1,0:T(8,128)(2,1)}) custom-call(s32[16]{0:T(128)} %len_hbm.1, f32[1,8192]{1,0:T(1,128)} %bitcast.4, f32[1,128]{1,0:T(1,128)} %constant.2.clone.freq_hbm, bf16[32,8192]{1,0:T(8,128)(2,1)} %bitcast.3, bf16[4096,1024]{1,0:T(8,128)(2,1)} %wq_hbm.1, bf16[4096,128]{1,0:T(8,128)(2,1)} %wk_hbm.1, ...), custom_call_target="tpu_custom_call" | custom-call | tf_op jit(solution)/shard_map/decode_block/pallas_call | solution.py:542
  43.0 1.5 %reshape.22 = bf16[2,16,2,512]{3,2,1,0:T(2,128)(2,1)} reshape(bf16[32,1024]{1,0:T(8,128)(2,1)} %get-tuple-element.5) | data formatting | bytes 131072 | tf_op jit(solution)/shard_map/reshape | solution.py:588
  44.5 1.4 %copy.13 = bf16[2,16,512]{2,1,0:T(8,128)(2,1)} copy(bf16[2,16,512]{2,1,0:T(8,128)(2,1)} %bitcast.5) | data formatting | bytes 65536

commit v4 on v2

--- a/solution.py
+++ b/solution.py
@@ -154,15 +154,17 @@
 MESH = pl.DeviceIdType.MESH
 LOW = -1e30
 CHUNKS = 8
+VMEM_BYTES = (64 * 1024 - 320) * 1024
 
 
 def block_kernel(
     n_gy,
-    len_ref, gain_ref, freq_ref, x_hbm, wq_hbm, wk_hbm, wv_hbm, wo_hbm, kc_hbm, vc_hbm,
+    len_hbm, gain_ref, freq_hbm, x_hbm, wq_hbm, wk_hbm, wv_hbm, wo_hbm, kc_hbm, vc_hbm,
     mixed_ref, fresh_ref,
+    len_ref, freq_ref,
     x_v, xn_v, w_v, wo_v, kc_v, vc_v, part, part_in, qsort, pack, gath, kvf,
     acc_s, acc_r, ml_s, ml_r, fresh_acc, att, flat, lhs, po_s, po_r,
-    sem_x, sem_wq, sem_wk, sem_wv, sem_kc, sem_vc, sem_wo,
+    sem_len, sem_freq, sem_x, sem_wq, sem_wk, sem_wv, sem_kc, sem_vc, sem_wo,
     pair_s, pair_r, gath_s, gath_r, accs, accr, mls, mlr, atts, attr, out_s, out_r,
 ):
     gx = lax.axis_index("gx")
@@ -186,6 +188,10 @@
 
     copy_x = pltpu.make_async_copy(x_hbm, x_v, sem_x)
     copy_x.start()
+    copy_len = pltpu.make_async_copy(len_hbm, len_ref, sem_len)
+    copy_len.start()
+    copy_freq = pltpu.make_async_copy(freq_hbm, freq_ref, sem_freq)
+    copy_freq.start()
 
     def wq_copies(c):
         r = pl.ds(c * step_rows, step_rows)
@@ -230,6 +236,9 @@
     for p in range(2):
         for c in range(4):
             wo_copy(p, c).start()
+
+    copy_len.wait()
+    copy_freq.wait()
 
     row16 = lax.broadcasted_iota(jnp.int32, (2 * hb, HD), 0)
     lane16 = lax.broadcasted_iota(jnp.int32, (2 * hb, HD), 1)
@@ -334,28 +343,33 @@
             copy.wait()
         owner = owner_of(d)
         ml = jnp.zeros((nqr, HD), jnp.float32)
-        for i in range(own):
-            b = owner * own + i
-            c = b // hb
-            bl = lax.rem(b, hb)
-            seen = lane_s < len_ref[b]
-            for h in range(heads):
-                k = i * heads + h
-                q = gath[h * 2 + c, pl.ds(pl.multiple_of(bl * nqr, nqr), nqr), :]
-                score = lax.dot_general(
-                    q, kc_v[d, i, :, h * HD : (h + 1) * HD], (((1,), (1,)), ((), ())),
-                    preferred_element_type=jnp.float32,
-                ) * scale
-                score = jnp.where(seen, score, LOW)
-                m = jnp.max(score, axis=1, keepdims=True)
-                p = jnp.where(seen, jnp.exp(score - m), 0.0)
-                o = jnp.dot(
-                    p.astype(jnp.bfloat16), vc_v[d, i, :, h * HD : (h + 1) * HD],
-                    preferred_element_type=jnp.float32,
-                )
-                acc_s[d, k * nqr : (k + 1) * nqr, :] = o.astype(jnp.bfloat16)
-                ml = jnp.where(lane_ml == k, m, ml)
-                ml = jnp.where(lane_ml == k + HD // 2, jnp.sum(p, axis=1, keepdims=True), ml)
+        ks = [(i, h) for i in range(own) for h in range(heads)]
+        rows_b = [owner * own + i for i in range(own)]
+        seen = [lane_s < len_ref[b] for b in rows_b]
+        scores = [
+            lax.dot_general(
+                gath[h * 2 + rows_b[i] // hb,
+                     pl.ds(pl.multiple_of(lax.rem(rows_b[i], hb) * nqr, nqr), nqr), :],
+                kc_v[d, i, :, h * HD : (h + 1) * HD], (((1,), (1,)), ((), ())),
+                preferred_element_type=jnp.float32,
+            )
+            for i, h in ks
+        ]
+        scores = [jnp.where(seen[i], s * scale, LOW) for (i, h), s in zip(ks, scores)]
+        peaks = [jnp.max(s, axis=1, keepdims=True) for s in scores]
+        probs = [jnp.where(seen[i], jnp.exp(s - m), 0.0) for (i, h), s, m in zip(ks, scores, peaks)]
+        outs = [
+            jnp.dot(
+                p.astype(jnp.bfloat16), vc_v[d, i, :, h * HD : (h + 1) * HD],
+                preferred_element_type=jnp.float32,
+            )
+            for (i, h), p in zip(ks, probs)
+        ]
+        sums = [jnp.sum(p, axis=1, keepdims=True) for p in probs]
+        for k in range(combos):
+            acc_s[d, k * nqr : (k + 1) * nqr, :] = outs[k].astype(jnp.bfloat16)
+            ml = jnp.where(lane_ml == k, peaks[k], ml)
+            ml = jnp.where(lane_ml == k + HD // 2, sums[k], ml)
         ml_s[d] = ml
 
         @pl.when(d < n_gy - 1)
@@ -498,16 +512,18 @@
     f32, b16 = jnp.float32, jnp.bfloat16
     dma = pltpu.SemaphoreType.DMA
     vmem = pl.BlockSpec(memory_space=pltpu.VMEM)
-    hbm = pl.BlockSpec(memory_space=pl.ANY)
+    hbm = pl.BlockSpec(memory_space=pltpu.HBM)
     mixed, fresh = pl.pallas_call(
         functools.partial(block_kernel, n_gy),
         out_shape=(
             jax.ShapeDtypeStruct((steps * rows, oc), b16),
             jax.ShapeDtypeStruct((steps * rows, 2 * kvl), b16),
         ),
-        in_specs=[pl.BlockSpec(memory_space=pltpu.SMEM), vmem, vmem] + [hbm] * 7,
+        in_specs=[hbm, vmem] + [hbm] * 8,
         out_specs=(vmem, vmem),
         scratch_shapes=[
+            pltpu.SMEM((rows,), jnp.int32),
+            pltpu.VMEM((1, HD), f32),
             pltpu.VMEM((steps * rows, width), b16),
             pltpu.VMEM((steps * rows, half), b16),
             pltpu.VMEM((half, qw + 2 * HD), b16),
@@ -530,13 +546,13 @@
             pltpu.VMEM((steps * rows, half), b16),
             pltpu.VMEM((steps * rows, oc), f32),
             pltpu.VMEM((steps * rows, oc), f32),
-            dma, dma((CHUNKS,)), dma((CHUNKS,)), dma((CHUNKS,)), dma((n_gy,)), dma((n_gy,)), dma((8,)),
+            dma, dma, dma, dma((CHUNKS,)), dma((CHUNKS,)), dma((CHUNKS,)), dma((n_gy,)), dma((n_gy,)), dma((8,)),
             dma, dma, dma((n_gy,)), dma((2 * heads,)),
             dma((n_gy - 1,)), dma((n_gy - 1,)), dma((n_gy - 1,)), dma((n_gy - 1,)),
             dma((n_gy - 1,)), dma((n_gy,)), dma, dma,
         ],
         compiler_params=pltpu.CompilerParams(
-            collective_id=0, has_side_effects=True, vmem_limit_bytes=52 * 1024 * 1024
+            collective_id=0, has_side_effects=True, vmem_limit_bytes=VMEM_BYTES
         ),
         name="decode_block",
     )(

time: 50.1 us -> 43.3 us (0.86)
  Pallas kernels: 43.6 us -> 38.1 us
  local copies, waits for them, and re-layouts: 4.85 us -> 2.87 us
  other arithmetic: 0.72 us -> 1.34 us
    pallas_call x1, Pallas kernels: 43.6 us -> 38.1 us  [on_device_kernel(): pl.pallas_call(functools.partial(block_kernel, n_gy), out_shape=(jax.Shap...]
    unnamed x9 -> x1, local copies, waits for them, and re-layouts: 4.19 us -> 1.37 us
    reshape x1, local copies, waits for them, and re-layouts: 0.66 us -> 1.5 us  [on_device_kernel(): return (mixed.reshape(steps, rows, oc), fresh.reshape(steps, rows, 2, kvl))]
    reshape x1, other arithmetic: 0.72 us -> 1.34 us  [on_device_kernel(): norm_gain.astype(f32).reshape(1, width)]
where the time goes in v4:
time: 43.3 us; the launch traced here: 43 us
  Pallas kernels  38.1 us (88%)
  local copies, waits for them, and re-layouts  2.87 us (7%)
  other arithmetic  1.34 us (3%)
  between operations  0.64 us (1%)
    pallas_call x1, Pallas kernels, on_device_kernel(): pl.pallas_call(functools.partial(block_kernel, n_gy), out_shape=(jax.Shap...  38.1 us
    reshape x1, local copies, waits for them, and re-layouts, on_device_kernel(): return (mixed.reshape(steps, rows, oc), fresh.reshape(steps, rows, 2, kvl))  1.5 us
    unnamed x1, local copies, waits for them, and re-layouts  1.37 us
    reshape x1, other arithmetic, on_device_kernel(): norm_gain.astype(f32).reshape(1, width)  1.34 us

profile of v4, /device:TPU:0, one launch (start us, length us, event | category | flops | bytes accessed | tf_op | source)
XLA Modules:
  0.0 43.0 jit_solution(6248517389935691197)
XLA Ops:
  0.6 1.3 %reshape.23 = f32[8192]{0:T(1024)} convert(bf16[8192]{0:T(1024)(128)(2,1)} %param.11) | non-fusion elementwise | flops 8192 | bytes 49152 | tf_op jit(solution)/shard_map/reshape | solution.py:559
  2.0 38.1 %decode_block.1 = (bf16[32,512]{1,0:T(8,128)(2,1)}, bf16[32,1024]{1,0:T(8,128)(2,1)}) custom-call(s32[16]{0:T(128)} %len_hbm.1, f32[1,8192]{1,0:T(1,128)} %bitcast.4, f32[1,128]{1,0:T(1,128)} %constant.2.clone.freq_hbm, bf16[32,8192]{1,0:T(8,128)(2,1)} %bitcast.3, bf16[4096,1024]{1,0:T(8,128)(2,1)} %wq_hbm.1, bf16[4096,128]{1,0:T(8,128)(2,1)} %wk_hbm.1, ...), custom_call_target="tpu_custom_call" | custom-call | tf_op jit(solution)/shard_map/decode_block/pallas_call | solution.py:516
  40.1 1.5 %reshape.22 = bf16[2,16,2,512]{3,2,1,0:T(2,128)(2,1)} reshape(bf16[32,1024]{1,0:T(8,128)(2,1)} %get-tuple-element.5) | data formatting | bytes 131072 | tf_op jit(solution)/shard_map/reshape | solution.py:562
  41.6 1.4 %copy.13 = bf16[2,16,512]{2,1,0:T(8,128)(2,1)} copy(bf16[2,16,512]{2,1,0:T(8,128)(2,1)} %bitcast.5) | data formatting | bytes 65536
